TPU v7x, 256 devices: a whole 4x4x8 slice. The times are simulated.
256 devices in a mesh: row: 16 (over y, z_lo, core), col: 4 (over x), chan: 4 (over z_hi).
Axes of the slice: x: 4, y: 4, z: 8 (z_hi: 4, z_lo: 2; z = z_hi * 2 + z_lo), core: 2. Of those that a mesh axis runs over, the one named last changes fastest.
Arguments:
- pair: bfloat16 [128, 512, 512], P('chan', 'row', 'col'), may hold values from -6 to 6
- token_valid: int32 [512], replicated, may hold values from 0 to 1, as said below
- ln_gain: float32 [128], replicated, may hold values from 0.5 to 1.5
- ln_bias: float32 [128], replicated, may hold values from -3 to 3
- w_agate: bfloat16 [128, 128], P(None, 'chan'), may hold values from -0.5 to 0.5
- w_aproj: bfloat16 [128, 128], P(None, 'chan'), may hold values from -0.5 to 0.5
- w_bgate: bfloat16 [128, 128], P(None, 'chan'), may hold values from -0.5 to 0.5
- w_bproj: bfloat16 [128, 128], P(None, 'chan'), may hold values from -0.5 to 0.5
- w_gate: bfloat16 [128, 128], P(None, 'chan'), may hold values from -0.5 to 0.5
- out_gain: float32 [128], P('chan'), may hold values from 0.5 to 1.5
- out_bias: float32 [128], P('chan'), may hold values from -3 to 3
- w_out: bfloat16 [128, 128], replicated, may hold values from -0.5 to 0.5
Outputs:
- update: bfloat16 [128, 512, 512], P('chan', 'row', 'col')
Inputs may be any that keep to these rules, and one draw needn't show every extreme that they name: token_valid is 1 for the first tokens of the complex and 0 for the padding after them; at least 256 tokens are real and the last token is padding.
All inputs are finite; a program needn't handle non-finite values.
Results may differ from a plain program's by a relative error of at most 0.015.
Values may be sent and summed in bfloat16 or wider, within the bound.
A program may use at most 64 MiB of HBM per device.

v0:
```python
import jax
import jax.numpy as jnp
from jax import lax
from jax.sharding import PartitionSpec as P

EPSILON = 1e-05


def spread(value, axis, source):
    kept = jnp.where(lax.axis_index(axis) == source, value, 0).astype(value.dtype)
    return lax.psum(kept, axis)


def layer_norm(values, gain, shift):
    centre = jnp.mean(values, axis=0, keepdims=True)
    spread_sq = jnp.mean(jnp.square(values - centre), axis=0, keepdims=True)
    return (values - centre) * lax.rsqrt(spread_sq + EPSILON) * gain[:, None, None] + shift[
        :, None, None
    ]


def on_device(
    pair,
    token_valid,
    ln_gain,
    ln_bias,
    w_agate,
    w_aproj,
    w_bgate,
    w_bproj,
    w_gate,
    out_gain,
    out_bias,
    w_out,
):
    chan_width, tile_rows, tile_cols = pair.shape
    row_devices = lax.axis_size("row")
    col_devices = lax.axis_size("col")
    row_begin = lax.axis_index("row") * tile_rows
    col_begin = lax.axis_index("col") * tile_cols
    row_valid = lax.dynamic_slice_in_dim(token_valid, row_begin, tile_rows).astype(jnp.float32)
    col_valid = lax.dynamic_slice_in_dim(token_valid, col_begin, tile_cols).astype(jnp.float32)
    gathered = lax.all_gather(pair, "chan", axis=0, tiled=True)
    full_width = gathered.shape[0]
    normed = layer_norm(gathered.astype(jnp.float32), ln_gain, ln_bias).astype(jnp.bfloat16)
    weights = jnp.concatenate([w_agate, w_aproj, w_bgate, w_bproj, w_gate], axis=1)
    projected_all = jnp.einsum(
        "crq,cd->drq", normed, weights, preferred_element_type=jnp.float32
    ).reshape(5, chan_width, tile_rows, tile_cols)
    pair_mask = (row_valid[:, None] * col_valid[None, :])[None, :, :]
    left_side = (jax.nn.sigmoid(projected_all[0]) * projected_all[1] * pair_mask).astype(
        jnp.bfloat16
    )
    right_side = (jax.nn.sigmoid(projected_all[2]) * projected_all[3] * pair_mask).astype(
        jnp.bfloat16
    )
    gate_value = jax.nn.sigmoid(projected_all[4]).astype(jnp.bfloat16)
    left_rows = lax.all_gather(left_side, "col", axis=2, tiled=True)
    right_rows = lax.all_gather(right_side, "col", axis=2, tiled=True)
    group_count = max(1, row_devices // col_devices)
    first_root = col_begin // tile_rows
    row_offset = col_begin % tile_rows
    pieces_list = []
    for member in range(group_count):
        panel = spread(right_rows, "row", first_root + member)
        pieces_list.append(
            jnp.einsum("cik,cjk->cij", left_rows, panel, preferred_element_type=jnp.float32)
        )
    mixed = jnp.concatenate(pieces_list, axis=2)
    first_sum, second_sum = (
        lax.psum(jnp.sum(mixed, axis=0).astype(jnp.bfloat16), "chan").astype(jnp.float32),
        lax.psum(jnp.sum(mixed * mixed, axis=0).astype(jnp.bfloat16), "chan").astype(jnp.float32),
    )
    centre = first_sum / full_width
    spread_sq = second_sum / full_width - centre * centre
    normed_mixed = (
        (mixed - centre) * lax.rsqrt(spread_sq + EPSILON) * out_gain[:, None, None]
        + out_bias[:, None, None]
    ).astype(jnp.bfloat16)
    chan_begin = lax.axis_index("chan") * chan_width
    whole_normed = lax.all_gather(normed_mixed, "chan", axis=0, tiled=True)
    out_columns = lax.dynamic_slice_in_dim(w_out, chan_begin, chan_width, 1)
    projected = jnp.einsum(
        "crq,cd->drq", whole_normed, out_columns, preferred_element_type=jnp.float32
    )
    return (gate_value.astype(jnp.float32) * projected).astype(jnp.bfloat16)


def solution(mesh):
    return jax.shard_map(
        on_device,
        mesh=mesh,
        in_specs=(
            P("chan", "row", "col"),
            P(),
            P(),
            P(),
            P(None, "chan"),
            P(None, "chan"),
            P(None, "chan"),
            P(None, "chan"),
            P(None, "chan"),
            P("chan"),
            P("chan"),
            P(),
        ),
        out_specs=P("chan", "row", "col"),
        check_vma=False,
    )
```

profile of v0, /device:TPU:1, one launch (start us, length us, event | category | flops | bytes accessed | tf_op | source)
XLA Modules:
  0.0 322.8 jit_solution(3669705686841184953)
XLA Ops:
  6.5 0.7 all-gather.5.cloned.1.call-update
  7.3 0.8 dynamic-slice_convert_fusion
  8.1 0.8 dynamic-slice_convert_fusion.1
  9.5 0.7 constant_dynamic-update-slice_fusion.3
  10.2 0.7 constant_dynamic-update-slice_fusion.2
  10.9 0.7 constant_dynamic-update-slice_fusion.1
  11.6 0.7 constant_dynamic-update-slice_fusion
  12.4 35.4 %all-gather.5.cloned.1.call-done = bf16[128,32,128]{2,1,0:T(8,128)(2,1)} async-done(((bf16[32,32,128]{2,1,0:T(8,128)(2,1)}), bf16[128,32,128]{2,1,0:T(8,128)(2,1)}) %all-gather.5.cloned.1.call-update) | async-done | bytes 1048592 | tf_op jit(solution)/shard_map/all_gather | solution.py:43
  47.8 1.5 convert_reduce_fusion
  49.3 1.6 fusion.2
  51.9 1.1 fusion.28
  53.8 25.0 %all-gather.9.cloned.1.call-done = bf16[32,32,512]{2,0,1:T(8,128)(2,1)} async-done(((bf16[32,32,128]{2,0,1:T(8,128)(2,1)}), bf16[32,32,512]{2,0,1:T(8,128)(2,1)}) %all-gather.9.cloned.1.call-update) | async-done | bytes 1048592 | tf_op jit(solution)/shard_map/all_gather | solution.py:59
  78.8 3.3 %broadcast_select_fusion.3 = (bf16[32,32,512]{2,0,1:T(8,128)(2,1)}, bf16[32,32,512]{2,0,1:T(8,128)(2,1)}, bf16[32,32,512]{2,0,1:T(8,128)(2,1)}, bf16[32,32,512]{2,0,1:T(8,128)(2,1)}) fusion(bf16[32,32,512]{2,0,1:T(8,128)(2,1)} %all-gather.9.cloned.1.call-done, pred[]{:T(512)S(6)} %eq.12, pred[]{:T(512)S(6)} %eq.15, pred[]{:T(512)S(6)} %eq.14, pred[]{:T(512)S(6)} %eq.13), kind=kLoop, calls=%fused_computation.24 | loop fusion | flops 2097152 | bytes 5242884 | tf_op jit(solution)/shard_map/jit(_where)/select_n | solution.py:10
  82.2 27.9 %all-gather.7.cloned.1.call-done = bf16[32,32,512]{2,0,1:T(8,128)(2,1)} async-done(((bf16[32,32,128]{2,0,1:T(8,128)(2,1)}), bf16[32,32,512]{2,0,1:T(8,128)(2,1)}) %all-gather.7.cloned.1.call-update) | async-done | bytes 1048592 | tf_op jit(solution)/shard_map/all_gather | solution.py:58
  110.1 143.8 %all-reduce.4.cloned.1.call-done = (bf16[32,32,512]{2,0,1:T(8,128)(2,1)}, bf16[32,32,512]{2,0,1:T(8,128)(2,1)}, bf16[32,32,512]{2,0,1:T(8,128)(2,1)}, bf16[32,32,512]{2,0,1:T(8,128)(2,1)}) async-done(((bf16[32,32,512]{2,0,1:T(8,128)(2,1)}, bf16[32,32,512]{2,0,1:T(8,128)(2,1)}, bf16[32,32,512]{2,0,1:T(8,128)(2,1)}, bf16[32,32,512]{2,0,1:T(8,128)(2,1)}), (bf16[32,32,512]{2,0,1:T(8,128)(2,1)}, ...) | async-done | bytes 4194320 | tf_op jit(solution)/shard_map/psum | solution.py:11
  253.9 2.9 fusion.14
  256.8 1.2 fusion.12
  258.1 1.2 fusion.10
  259.3 1.2 fusion.8
  261.0 16.0 %all-reduce.1 = (bf16[32,128]{1,0:T(8,128)(2,1)S(1)}, bf16[32,128]{1,0:T(8,128)(2,1)S(1)}) all-reduce(bf16[32,128]{1,0:T(8,128)(2,1)S(1)} %get-tuple-element.6, bf16[32,128]{1,0:T(8,128)(2,1)S(1)} %get-tuple-element.5), channel_id=1, replica_groups=mesh['row'=16,'col'=4,'chan'=4] {'chan'}, use_global_device_ids=true, to_apply=%region_9.10 | all-reduce | flops 8192 | bytes 32768 | tf_op jit(solution)/shard_map/psum | solution.py:72
  277.0 0.9 add_convert_fusion
  277.9 35.8 %all-gather.11.cloned.1.call-done = bf16[128,32,128]{2,1,0:T(8,128)(2,1)} async-done(((bf16[32,32,128]{2,1,0:T(8,128)(2,1)}), bf16[128,32,128]{2,1,0:T(8,128)(2,1)}) %all-gather.11.cloned.1.call-update) | async-done | bytes 1048592 | tf_op jit(solution)/shard_map/all_gather | solution.py:81
  313.7 1.7 fusion.6
  315.5 0.8 copy.36
  (37 shorter events, 3.2 us)
Async XLA Ops:
  6.5 307.2 %copy-start = (bf16[128,128]{1,0:T(8,128)(2,1)S(1)}, bf16[128,128]{1,0:T(8,128)(2,1)}, u32[]{:S(2)}) copy-start(bf16[128,128]{1,0:T(8,128)(2,1)} %param.23) | copy-start | bytes 98308
  6.5 44.3 %copy-start.5 = (f32[128]{0:T(128)S(1)}, f32[128]{0:T(128)}, u32[]{:S(2)}) copy-start(f32[128]{0:T(128)} %param.14) | copy-start | bytes 1540
  6.5 44.3 %copy-start.4 = (f32[128]{0:T(128)S(1)}, f32[128]{0:T(128)}, u32[]{:S(2)}) copy-start(f32[128]{0:T(128)} %param.15) | copy-start | bytes 1540
  6.5 41.2 %all-gather.5.cloned.1.call-start = ((), (), s32[]{:S(2)}) async-start(), calls=%async_computation | async-start | bytes 1310720 | tf_op jit(solution)/shard_map/all_gather | solution.py:43
  7.3 71.6 %all-gather.9.cloned.1.call-start = ((), (), s32[]{:S(2)}) async-start(), calls=%async_computation.2 | async-start | bytes 1310720 | tf_op jit(solution)/shard_map/all_gather | solution.py:59
  47.8 3.1 copy-start.1
  53.0 57.1 %all-gather.7.cloned.1.call-start = ((), (), s32[]{:S(2)}) async-start(), calls=%async_computation.1 | async-start | bytes 1310720 | tf_op jit(solution)/shard_map/all_gather | solution.py:58
  53.7 200.2 %all-reduce.4.cloned.1.call-start = ((), (), s32[]{:S(2)}) async-start(), calls=%async_computation.4 | async-start | bytes 8388608 | tf_op jit(solution)/shard_map/psum | solution.py:11
  82.1 231.6 %all-gather.11.cloned.1.call-start = ((), (), s32[]{:S(2)}) async-start(), calls=%async_computation.3 | async-start | bytes 1310720 | tf_op jit(solution)/shard_map/all_gather | solution.py:81
  253.9 2.9 copy-start.6
  253.9 2.9 copy-start.9
  256.8 1.2 copy-start.8
  258.1 1.2 copy-start.7
  260.5 16.5 %copy-start.2 = (f32[32]{0:T(128)S(1)}, f32[32]{0:T(128)}, u32[]{:S(2)}) copy-start(f32[32]{0:T(128)} %param.22) | copy-start | bytes 388
  260.5 16.5 %copy-start.3 = (f32[32]{0:T(128)S(1)}, f32[32]{0:T(128)}, u32[]{:S(2)}) copy-start(f32[32]{0:T(128)} %param.21) | copy-start | bytes 388
Sparse Core Ops, SparseCore 0:
  9.2 38.5 all-gather.4
  53.1 25.6 all-gather.8
  80.6 29.3 all-gather.6
  112.8 141.0 all-reduce.3
  278.0 35.6 all-gather.10
where the time goes:
time: 323 us
  waiting for transfers between devices  269 us (83%)
  blocking collectives  16 us (5%)
  between operations  13.3 us (4%)
  other arithmetic  10.8 us (3%)
  matrix products  8.83 us (3%)
  local copies, waits for them, and re-layouts  4.36 us (1%)
    psum x1, waiting for transfers between devices, spread(): return lax.psum(kept, axis)  144 us
    all_gather x1, waiting for transfers between devices, on_device(): whole_normed = lax.all_gather(normed_mixed, 'chan', axis=0, tiled=True)  35.8 us
    all_gather x1, waiting for transfers between devices, on_device(): gathered = lax.all_gather(pair, 'chan', axis=0, tiled=True)  35.4 us
    all_gather x1, waiting for transfers between devices, on_device(): left_rows = lax.all_gather(left_side, 'col', axis=2, tiled=True)  27.9 us
    all_gather x1, waiting for transfers between devices, on_device(): right_rows = lax.all_gather(right_side, 'col', axis=2, tiled=True)  25 us
    psum x1, blocking collectives, on_device(): lax.psum(jnp.sum(mixed * mixed, axis=0).astype(jnp.bfloat16), 'chan')  16 us
    dot_general x4, matrix products, on_device(): jnp.einsum('cik,cjk->cij', left_rows, panel, preferred_element_type=jnp.f...  6.55 us
  transfers between devices with their start and end apart: 5, of which 5 were waited for; matrix products, arithmetic and copies ran while one was open for 3% of the time, Pallas kernels for 0%

commit v1 on v0

v1 whole, which is shorter than its diff:
```python
import jax
import jax.numpy as jnp
from jax import lax
from jax.experimental import pallas as pl
from jax.experimental.pallas import tpu as pltpu
from jax.sharding import PartitionSpec as P

EPSILON = 1e-05
MESH = pl.DeviceIdType.MESH
F32 = jnp.float32
BF16 = jnp.bfloat16
NT = (((1,), (1,)), ((), ()))


def device_at(x, y, z, core):
    return ((y * 2 + z % 2) * 2 + core, x, z // 2)


def wait_bytes(ref, sem):
    pltpu.make_async_copy(ref, ref, sem).wait()


def remote(src, dst, send_sem, recv_sem, device):
    return pltpu.make_async_remote_copy(
        src, dst, send_sem, recv_sem, device_id=device, device_id_type=MESH
    )


def rows_of(block):
    return block.astype(F32).reshape(-1, 128).astype(BF16)


def one_hot(shape, offset):
    first = lax.broadcasted_iota(jnp.int32, shape, 0)
    second = lax.broadcasted_iota(jnp.int32, shape, 1)
    return (second == first + offset).astype(F32).astype(BF16)


def centred(blocks, scratch, gain=None, shift=None):
    def add(step, total):
        part = blocks[step].astype(F32)
        return total + jnp.sum(part, axis=0)

    centre = lax.fori_loop(0, 8, add, jnp.zeros((8, 128), F32)) * (1.0 / 128)

    def add_square(step, total):
        part = blocks[step].astype(F32) - centre
        return total + jnp.sum(part * part, axis=0)

    spread = lax.fori_loop(0, 8, add_square, jnp.zeros((8, 128), F32)) * (1.0 / 128)
    scale = lax.rsqrt(spread + EPSILON)

    def put(step, _):
        for member in range(16):
            c = step * 16 + member
            value = (blocks[step, member].astype(F32) - centre) * scale
            if gain is not None:
                value = value * gain[c] + shift[c]
            scratch[pl.ds(pl.multiple_of(c * 8, 8), 8), :] = value
        return 0

    lax.fori_loop(0, 8, put, 0)


def by_channel(scratch, out):
    def put(step, _):
        for member in range(16):
            out[step, member] = scratch[pl.ds(step * 16 + member, 8, stride=128), :].astype(BF16)
        return 0

    lax.fori_loop(0, 8, put, 0)


def kernel(
    pair, valid_row, valid_s_in, gain_in, bias_in, w0, w1, w2, w3, w4, out_gain_in, out_bias_in, w_out_in,
    out,
    xin, valid_v, valid_s, gain_s, bias_s, out_gain_s, out_bias_s, w_v, w_out_v, w_all, w_out_t,
    edge, edge_all,
    wide, left_f, right_f, gate_f,
    left_send, left_mid, left_all, right_send, right_mid, right_all,
    mixed_send, mixed_mid, mixed_all, out_send,
    load_sem, send_sem, recv_sem, own_sem, sibling_send, right_recv, sibling_recv,
):
    row, x, z_hi = lax.axis_index("row"), lax.axis_index("col"), lax.axis_index("chan")
    core, z_lo, y = row % 2, (row // 2) % 2, row // 4
    z = z_hi * 2 + z_lo
    xy = y * 4 + x

    def z_peer(t):
        return lax.rem(z + t, 8)

    def hi_peer(t):
        return lax.rem(z_hi + t, 4)

    def xy_peer(t):
        px, py = lax.rem(x + t % 4, 4), lax.rem(y + t // 4, 4)
        return px, py

    def at_z(pz):
        return device_at(x, y, pz, core)

    def at_hi(ph):
        return (row, x, ph)

    def at_xy(px, py):
        return device_at(px, py, z, core)

    sibling = device_at(x, y, z, 1 - core)

    barrier = pltpu.get_barrier_semaphore()

    def greet_z(t, _):
        pl.semaphore_signal(barrier, inc=1, device_id=at_z(z_peer(t)), device_id_type=MESH)
        return 0

    def greet_xy(t, _):
        pl.semaphore_signal(barrier, inc=1, device_id=at_xy(*xy_peer(t)), device_id_type=MESH)
        return 0

    lax.fori_loop(1, 8, greet_z, 0)
    lax.fori_loop(1, 16, greet_xy, 0)
    pl.semaphore_signal(barrier, inc=1, device_id=sibling, device_id_type=MESH)

    own_rows = pltpu.make_async_copy(pair.at[:, :, z_hi], xin.at[pl.ds(z_hi * 2, 2)], load_sem.at[0])
    own_rows.start()
    weight_loads = []
    for t, w in enumerate((w0, w1, w2, w3, w4)):
        weight_loads.append(pltpu.make_async_copy(w, w_v.at[t], load_sem.at[1 + t]))
    weight_loads.append(pltpu.make_async_copy(w_out_in, w_out_v, load_sem.at[6]))
    small_loads = [
        pltpu.make_async_copy(valid_row, valid_v, load_sem.at[7]),
        pltpu.make_async_copy(valid_s_in, valid_s, load_sem.at[8]),
        pltpu.make_async_copy(gain_in, gain_s, load_sem.at[9]),
        pltpu.make_async_copy(bias_in, bias_s, load_sem.at[10]),
        pltpu.make_async_copy(out_gain_in, out_gain_s, load_sem.at[11]),
        pltpu.make_async_copy(out_bias_in, out_bias_s, load_sem.at[12]),
    ]
    for copy in weight_loads + small_loads:
        copy.start()

    pl.semaphore_wait(barrier, 23)

    for t in (2, 1, 3):
        ph = hi_peer(t)
        remote(
            pair.at[:, :, ph], xin.at[pl.ds(z_hi * 2, 2)], send_sem.at[0], recv_sem.at[0], at_hi(ph)
        ).start()

    for copy in weight_loads + small_loads:
        copy.wait()
    pick = one_hot((16, 32), x * 8)
    for t in range(5):
        turned = lax.dot_general(pick, w_v[t], NT, preferred_element_type=F32)
        w_all[t, z_hi, x] = turned[0:8].astype(BF16)
    lane = lax.broadcasted_iota(jnp.int32, (8, 128), 1)
    line = lax.broadcasted_iota(jnp.int32, (8, 128), 0)

    def put_edge(i, held):
        value = jnp.where(line == 0, out_gain_s[i], out_bias_s[i])
        return jnp.where(lane == z_hi * 32 + i, value, held)

    edge[...] = lax.fori_loop(0, 32, put_edge, jnp.zeros((8, 128), F32))
    for t in (1, 2, 3):
        ph = hi_peer(t)
        remote(
            w_all.at[:, z_hi, x], w_all.at[:, z_hi, x], send_sem.at[1], recv_sem.at[1], at_hi(ph)
        ).start()
        remote(edge, edge_all.at[z_hi], send_sem.at[2], recv_sem.at[2], at_hi(ph)).start()
    edge_all[z_hi] = edge[...]
    w_out_t[...] = lax.dot_general(
        one_hot((128, 128), 0), w_out_v[...], NT, preferred_element_type=F32
    ).astype(BF16)
    wait_bytes(w_all.at[:, 0, pl.ds(0, 3)], recv_sem.at[1])
    for t in (1, 2, 3):
        px = lax.rem(x + t, 4)
        remote(
            w_all.at[:, :, x], w_all.at[:, :, x], send_sem.at[3], recv_sem.at[3], at_xy(px, y)
        ).start()
    wait_bytes(edge_all.at[pl.ds(0, 3)], recv_sem.at[2])
    edge_sum = edge_all[0] + edge_all[1] + edge_all[2] + edge_all[3]
    out_gain = jnp.transpose(jnp.broadcast_to(edge_sum[0:1], (128, 128)))
    out_shift = jnp.transpose(jnp.broadcast_to(edge_sum[1:2], (128, 128)))

    own_rows.wait()
    wait_bytes(xin.at[pl.ds(0, 6)], recv_sem.at[0])
    centred(xin, wide, gain_s, bias_s)

    wait_bytes(w_all.at[:, :, pl.ds(0, 3)], recv_sem.at[3])
    col_valid = valid_v[pl.ds(x, 1), :].astype(F32)
    first_row = row * 32 + z_hi * 8

    def project(step, _):
        normed, masks = [], []
        for member in range(2):
            r = step * 2 + member
            normed.append(wide[pl.ds(r, 128, stride=8), :].astype(BF16))
            masks.append(col_valid * valid_s[first_row + r].astype(F32))
        normed = jnp.concatenate(normed, axis=1)
        mask = jnp.concatenate(masks, axis=1)

        def linear(t):
            return jnp.dot(rows_of(w_all[t]), normed, preferred_element_type=F32)

        left = jax.nn.sigmoid(linear(0)) * linear(1) * mask
        right = jax.nn.sigmoid(linear(2)) * linear(3) * mask
        gate = jax.nn.sigmoid(linear(4)).astype(BF16).astype(F32)
        for member in range(2):
            at = pl.ds(pl.multiple_of((step * 2 + member) * 128, 128), 128)
            lanes = slice(member * 128, member * 128 + 128)
            left_f[at, :] = left[:, lanes]
            right_f[at, :] = right[:, lanes]
            gate_f[at, :] = gate[:, lanes]
        return 0

    lax.fori_loop(0, 4, project, 0)
    by_channel(right_f, right_send)

    def send_right(t, _):
        px, py = xy_peer(t)
        remote(
            right_send.at[:, py * 4 + px], right_mid.at[xy], send_sem.at[4], recv_sem.at[4], at_xy(px, py)
        ).start()
        return 0

    def own(src, dst, i):
        copy = pltpu.make_async_copy(src, dst, own_sem.at[i])
        copy.start()
        return copy

    lax.fori_loop(1, 16, send_right, 0)
    own_right = own(right_send.at[:, xy], right_mid.at[xy], 0)
    by_channel(left_f, left_send)

    def send_left(t, _):
        pz = z_peer(t)
        remote(
            left_send.at[pz], left_mid.at[z], send_sem.at[5], recv_sem.at[5], at_z(pz)
        ).start()
        return 0

    lax.fori_loop(1, 8, send_left, 0)
    own_left = own(left_send.at[z], left_mid.at[z], 1)

    own_right.wait()
    wait_bytes(right_mid.at[pl.ds(0, 15)], recv_sem.at[4])

    def slot(pz, pcore):
        return (pz % 2) * 8 + pcore * 4 + pz // 2

    mine = slot(z, core)

    def pass_right(t, _):
        pz = z_peer(t)
        remote(
            right_mid.at[:, pz], right_all.at[:, mine], send_sem.at[6], right_recv.at[8 - t], at_z(pz)
        ).start()
        return 0

    lax.fori_loop(1, 8, pass_right, 0)
    own_right = own(right_mid.at[:, z], right_all.at[:, mine], 2)

    own_left.wait()
    wait_bytes(left_mid.at[pl.ds(0, 7)], recv_sem.at[5])

    def pass_left(t, _):
        px, py = xy_peer(t)
        remote(
            left_mid.at[:, py * 4 + px], left_all.at[xy], send_sem.at[7], recv_sem.at[7], at_xy(px, py)
        ).start()
        return 0

    lax.fori_loop(1, 16, pass_left, 0)
    own_left = own(left_mid.at[:, xy], left_all.at[xy], 3)

    own_right.wait()

    def to_sibling(pz):
        part = right_all.at[:, slot(pz, core)]
        remote(part, part, sibling_send, sibling_recv, sibling).start()

    to_sibling(z)

    def share(t, _):
        wait_bytes(right_all.at[:, 0], right_recv.at[t])
        to_sibling(z_peer(t))
        return 0

    lax.fori_loop(1, 8, share, 0)
    own_left.wait()
    wait_bytes(left_all.at[pl.ds(0, 15)], recv_sem.at[7])
    wait_bytes(right_all.at[:, pl.ds(0, 8)], sibling_recv)

    for part in range(4):
        total = jnp.zeros((256, 128), F32)
        for step in range(4):
            left = jnp.concatenate([rows_of(left_all[py * 4 + step]) for py in range(4)], axis=0)
            right = rows_of(right_all[part * 4 + step])
            total = total + lax.dot_general(left, right, NT, preferred_element_type=F32)
        for py in range(4):
            mixed_send[:, py * 4 + part] = (
                total[py * 64 : py * 64 + 64].reshape(8, 8, 128).astype(BF16)
            )

    def send_mixed(t, _):
        pz = z_peer(t)
        remote(
            mixed_send.at[pz], mixed_mid.at[z], send_sem.at[8], recv_sem.at[8], at_z(pz)
        ).start()
        return 0

    lax.fori_loop(1, 8, send_mixed, 0)
    own(mixed_send.at[z], mixed_mid.at[z], 4).wait()
    wait_bytes(mixed_mid.at[pl.ds(0, 7)], recv_sem.at[8])

    def pass_mixed(t, _):
        px, py = xy_peer(t)
        remote(
            mixed_mid.at[:, py * 4 + px], mixed_all.at[:, xy], send_sem.at[9], recv_sem.at[9], at_xy(px, py)
        ).start()
        return 0

    lax.fori_loop(1, 16, pass_mixed, 0)
    own(mixed_mid.at[:, xy], mixed_all.at[:, xy], 5).wait()
    wait_bytes(mixed_all.at[:, pl.ds(0, 15)], recv_sem.at[9])

    centred(mixed_all, wide)

    def finish(step, _):
        normed = []
        for member in range(2):
            r = step * 2 + member
            value = wide[pl.ds(r, 128, stride=8), :] * out_gain + out_shift
            normed.append(value.astype(BF16))
        projected = jnp.dot(
            w_out_t[...], jnp.concatenate(normed, axis=1), preferred_element_type=F32
        )
        for member in range(2):
            at = pl.ds(pl.multiple_of((step * 2 + member) * 128, 128), 128)
            left_f[at, :] = gate_f[at, :] * projected[:, member * 128 : member * 128 + 128]
        return 0

    lax.fori_loop(0, 4, finish, 0)
    by_channel(left_f, out_send)

    for t in (2, 1, 3):
        ph = hi_peer(t)
        remote(
            out_send.at[pl.ds(ph * 2, 2)], out.at[:, :, z_hi], send_sem.at[10], recv_sem.at[10], at_hi(ph)
        ).start()
    own(out_send.at[pl.ds(z_hi * 2, 2)], out.at[:, :, z_hi], 6).wait()
    wait_bytes(out.at[:, :, pl.ds(0, 3)], recv_sem.at[10])

    wait_bytes(xin.at[pl.ds(0, 6)], send_sem.at[0])
    wait_bytes(w_all.at[:, 0, pl.ds(0, 3)], send_sem.at[1])
    wait_bytes(edge_all.at[pl.ds(0, 3)], send_sem.at[2])
    wait_bytes(w_all.at[:, :, pl.ds(0, 3)], send_sem.at[3])
    wait_bytes(right_mid.at[pl.ds(0, 15)], send_sem.at[4])
    wait_bytes(left_mid.at[pl.ds(0, 7)], send_sem.at[5])
    wait_bytes(right_mid.at[:, pl.ds(0, 7)], send_sem.at[6])
    wait_bytes(left_all.at[pl.ds(0, 15)], send_sem.at[7])
    wait_bytes(mixed_mid.at[pl.ds(0, 7)], send_sem.at[8])
    wait_bytes(mixed_all.at[:, pl.ds(0, 15)], send_sem.at[9])
    wait_bytes(out.at[:, :, pl.ds(0, 3)], send_sem.at[10])
    wait_bytes(right_all.at[:, pl.ds(0, 8)], sibling_send)


def on_device(
    pair,
    token_valid,
    ln_gain,
    ln_bias,
    w_agate,
    w_aproj,
    w_bgate,
    w_bproj,
    w_gate,
    out_gain,
    out_bias,
    w_out,
):
    any_spec = pl.BlockSpec(memory_space=pl.ANY)
    result = pl.pallas_call(
        kernel,
        name="triangle",
        out_shape=jax.ShapeDtypeStruct((2, 16, 4, 8, 128), BF16),
        in_specs=[any_spec] * 13,
        out_specs=any_spec,
        scratch_shapes=[
            pltpu.VMEM((8, 16, 8, 128), BF16),
            pltpu.VMEM((4, 128), jnp.int32),
            pltpu.SMEM((512,), jnp.int32),
            pltpu.SMEM((128,), F32),
            pltpu.SMEM((128,), F32),
            pltpu.SMEM((32,), F32),
            pltpu.SMEM((32,), F32),
            pltpu.VMEM((5, 128, 32), BF16),
            pltpu.VMEM((128, 128), BF16),
            pltpu.VMEM((5, 4, 4, 8, 128), BF16),
            pltpu.VMEM((128, 128), BF16),
            pltpu.VMEM((8, 128), F32),
            pltpu.VMEM((4, 8, 128), F32),
            pltpu.VMEM((1024, 128), F32),
            pltpu.VMEM((1024, 128), F32),
            pltpu.VMEM((1024, 128), F32),
            pltpu.VMEM((1024, 128), F32),
            pltpu.VMEM((8, 16, 8, 128), BF16),
            pltpu.VMEM((8, 16, 8, 128), BF16),
            pltpu.VMEM((16, 8, 8, 128), BF16),
            pltpu.VMEM((8, 16, 8, 128), BF16),
            pltpu.VMEM((16, 8, 8, 128), BF16),
            pltpu.VMEM((16, 16, 8, 128), BF16),
            pltpu.VMEM((8, 16, 8, 128), BF16),
            pltpu.VMEM((8, 16, 8, 128), BF16),
            pltpu.VMEM((8, 16, 8, 128), BF16),
            pltpu.VMEM((8, 16, 8, 128), BF16),
            pltpu.SemaphoreType.DMA((13,)),
            pltpu.SemaphoreType.DMA((11,)),
            pltpu.SemaphoreType.DMA((11,)),
            pltpu.SemaphoreType.DMA((7,)),
            pltpu.SemaphoreType.DMA,
            pltpu.SemaphoreType.DMA((8,)),
            pltpu.SemaphoreType.DMA,
        ],
        compiler_params=pltpu.CompilerParams(
            collective_id=0, has_side_effects=True, vmem_limit_bytes=32 << 20
        ),
    )(
        pair.reshape(2, 16, 4, 8, 128),
        token_valid.reshape(4, 128),
        token_valid,
        ln_gain,
        ln_bias,
        w_agate,
        w_aproj,
        w_bgate,
        w_bproj,
        w_gate,
        out_gain,
        out_bias,
        w_out,
    )
    return result.reshape(32, 32, 128)


def solution(mesh):
    return jax.shard_map(
        on_device,
        mesh=mesh,
        in_specs=(
            P("chan", "row", "col"),
            P(),
            P(),
            P(),
            P(None, "chan"),
            P(None, "chan"),
            P(None, "chan"),
            P(None, "chan"),
            P(None, "chan"),
            P("chan"),
            P("chan"),
            P(),
        ),
        out_specs=P("chan", "row", "col"),
        check_vma=False,
    )
```

time: 323 us -> 70.8 us (0.22)
  waiting for transfers between devices: 269 us -> 0 us
  Pallas kernels: 0 us -> 65.2 us
  blocking collectives: 16 us -> 0 us
  between operations: 13.3 us -> 0.05 us
  other arithmetic: 10.8 us -> 0 us
  matrix products: 8.83 us -> 0 us
    psum x1 -> x0, waiting for transfers between devices: 144 us -> none  [spread(): return lax.psum(kept, axis)]
    all_gather x4 -> x0, waiting for transfers between devices: 124 us -> none  [the longest x1 35.8 us: on_device(): whole_normed = lax.all_gather(normed_mixed, 'chan', axis=0, tiled=True)]
    pallas_call x0 -> x1, Pallas kernels: none -> 65.2 us  [on_device(): pl.pallas_call(kernel, name='triangle', out_shape=jax.ShapeDtypeStruct((2...]
    psum x1 -> x0, blocking collectives: 16 us -> none  [on_device(): lax.psum(jnp.sum(mixed * mixed, axis=0).astype(jnp.bfloat16), 'chan')]
    dot_general x6 -> x0, matrix products: 8.83 us -> none  [the longest x4 6.55 us: on_device(): jnp.einsum('cik,cjk->cij', left_rows, panel, preferred_element_type=jnp.f...]
    convert_element_type x5 -> x0, other arithmetic: 3.92 us -> none  [the longest x1 1.1 us: on_device(): (jax.nn.sigmoid(projected_all[0]) * projected_all[1] * pair_mask).astype(...]
    reduce_sum x3 -> x0, other arithmetic: 3.55 us -> none  [the longest x1 1.55 us: layer_norm(): spread_sq = jnp.mean(jnp.square(values - centre), axis=0, keepdims=True)]
    select_n x1 -> x0, other arithmetic: 3.27 us -> none  [spread(): jnp.where(lax.axis_index(axis) == source, value, 0).astype(value.dtype)]
  transfers between devices with their start and end apart: 5 -> 0, of which waited for: 5 -> 0; matrix products, arithmetic and copies ran while one was open for 3% -> 0% of each run, Pallas kernels for 0% -> 0%
where the time goes in v1:
time: 70.8 us; the launch traced here: 70.5 us
  Pallas kernels  65.2 us (92%)
  local copies, waits for them, and re-layouts  5.27 us (7%)
    pallas_call x1, Pallas kernels, on_device(): pl.pallas_call(kernel, name='triangle', out_shape=jax.ShapeDtypeStruct((2...  65.2 us
    unnamed x28, local copies, waits for them, and re-layouts  5.27 us

profile of v1, /device:TPU:1, one launch (start us, length us, event | category | flops | bytes accessed | tf_op | source)
XLA Modules:
  0.0 70.5 jit_solution(16135011880980143042)
XLA Ops:
  0.0 0.0 copy-start.7
  0.0 0.8 %copy.13.w0 = bf16[128,32]{1,0:T(8,128)(2,1)S(1)} copy(bf16[128,32]{0,1:T(8,128)(2,1)} %param.16) | data formatting | bytes 16384 | tf_op args[4]
  0.8 0.0 copy-done.7
  0.8 0.0 copy-start.8
  0.8 0.1 copy.14.w1
  1.0 0.6 copy-done.8
  1.5 0.0 copy-start.9
  1.5 0.1 copy.15.w2
  1.7 0.6 copy-done.9
  2.2 0.0 copy-start.10
  2.2 0.0 copy-start.1
  2.2 0.1 copy.16.w3
  2.4 0.6 copy-done.10
  2.9 0.0 copy-start.6
  3.0 0.1 copy.17.w4
  3.1 0.0 copy-done.1
  3.1 0.5 copy-done.2
  3.6 0.0 copy-done.3
  3.6 0.0 copy-done.4
  3.6 0.0 copy-done.5
  3.6 0.0 copy-done.6
  3.7 0.9 %copy-done = bf16[32,32,128]{2,1,0:T(8,128)(2,1)S(1)} copy-done((bf16[32,32,128]{2,1,0:T(8,128)(2,1)S(1)}, bf16[32,32,128]{2,1,0:T(8,128)(2,1)}, u32[]{:S(2)}) %copy-start) | copy-done | bytes 262168
  4.6 65.2 %triangle.1 = bf16[2,16,4,8,128]{4,3,2,1,0:T(8,128)(2,1)S(1)} custom-call(bf16[2,16,4,8,128]{4,3,2,1,0:T(8,128)(2,1)S(1)} %bitcast.4, s32[4,128]{1,0:T(4,128)S(1)} %bitcast.5, s32[512]{0:T(512)S(1)} %copy-done.2, f32[128]{0:T(128)S(1)} %copy-done.3, f32[128]{0:T(128)S(1)} %copy-done.4, bf16[128,32]{1,0:T(8,128)(2,1)S(1)} %copy.13.w0, ...), custom_call_target="tpu_custom_call" | custom-call | tf_op jit(solution)/shard_map/triangle/pallas_call | solution.py:382
  69.8 0.7 %copy.19 = bf16[32,32,128]{2,1,0:T(8,128)(2,1)} copy(bf16[32,32,128]{2,1,0:T(8,128)(2,1)S(1)} %bitcast.3) | data formatting | bytes 524288
  (5 shorter events, 0.0 us)
Async XLA Ops:
  0.0 0.8 %copy-start.7 = (bf16[128,32]{0,1:T(8,128)(2,1)S(1)}, bf16[128,32]{0,1:T(8,128)(2,1)}, u32[]{:S(2)}) copy-start(bf16[128,32]{0,1:T(8,128)(2,1)} %param.17) | copy-start | bytes 24580
  0.8 0.7 copy-start.8
  1.5 0.7 copy-start.9
  2.2 0.7 copy-start.10
  2.2 0.8 %copy-start.1 = (bf16[128,128]{1,0:T(8,128)(2,1)S(1)}, bf16[128,128]{1,0:T(8,128)(2,1)}, u32[]{:S(2)}) copy-start(bf16[128,128]{1,0:T(8,128)(2,1)} %w_out_in.1) | copy-start | bytes 98308
  2.9 0.7 copy-start.2
  2.9 0.7 copy-start.3
  2.9 0.7 copy-start.4
  2.9 0.7 copy-start.5
  2.9 0.7 %copy-start.6 = (f32[32]{0:T(128)S(1)}, f32[32]{0:T(128)}, u32[]{:S(2)}) copy-start(f32[32]{0:T(128)} %out_bias_in.1) | copy-start | bytes 388
  3.6 0.9 %copy-start = (bf16[32,32,128]{2,1,0:T(8,128)(2,1)S(1)}, bf16[32,32,128]{2,1,0:T(8,128)(2,1)}, u32[]{:S(2)}) copy-start(bf16[32,32,128]{2,1,0:T(8,128)(2,1)} %param.12) | copy-start | bytes 786436

commit v2 on v1

--- a/solution.py
+++ b/solution.py
@@ -38,13 +38,13 @@
 
 def centred(blocks, scratch, gain=None, shift=None):
     def add(step, total):
-        part = blocks[step].astype(F32)
+        part = blocks[pl.ds(step * 16, 16)].astype(F32)
         return total + jnp.sum(part, axis=0)
 
     centre = lax.fori_loop(0, 8, add, jnp.zeros((8, 128), F32)) * (1.0 / 128)
 
     def add_square(step, total):
-        part = blocks[step].astype(F32) - centre
+        part = blocks[pl.ds(step * 16, 16)].astype(F32) - centre
         return total + jnp.sum(part * part, axis=0)
 
     spread = lax.fori_loop(0, 8, add_square, jnp.zeros((8, 128), F32)) * (1.0 / 128)
@@ -53,7 +53,7 @@
     def put(step, _):
         for member in range(16):
             c = step * 16 + member
-            value = (blocks[step, member].astype(F32) - centre) * scale
+            value = (blocks[c].astype(F32) - centre) * scale
             if gain is not None:
                 value = value * gain[c] + shift[c]
             scratch[pl.ds(pl.multiple_of(c * 8, 8), 8), :] = value
@@ -74,11 +74,11 @@
 def kernel(
     pair, valid_row, valid_s_in, gain_in, bias_in, w0, w1, w2, w3, w4, out_gain_in, out_bias_in, w_out_in,
     out,
-    xin, valid_v, valid_s, gain_s, bias_s, out_gain_s, out_bias_s, w_v, w_out_v, w_all, w_out_t,
+    xin, valid_v, valid_s, gain_s, bias_s, out_gain_s, out_bias_s, w_out_v, w_all, w_out_t,
     edge, edge_all,
     wide, left_f, right_f, gate_f,
     left_send, left_mid, left_all, right_send, right_mid, right_all,
-    mixed_send, mixed_mid, mixed_all, out_send,
+    mixed_send, mixed_all, out_send,
     load_sem, send_sem, recv_sem, own_sem, sibling_send, right_recv, sibling_recv,
 ):
     row, x, z_hi = lax.axis_index("row"), lax.axis_index("col"), lax.axis_index("chan")
@@ -121,37 +121,26 @@
     lax.fori_loop(1, 16, greet_xy, 0)
     pl.semaphore_signal(barrier, inc=1, device_id=sibling, device_id_type=MESH)
 
-    own_rows = pltpu.make_async_copy(pair.at[:, :, z_hi], xin.at[pl.ds(z_hi * 2, 2)], load_sem.at[0])
-    own_rows.start()
-    weight_loads = []
-    for t, w in enumerate((w0, w1, w2, w3, w4)):
-        weight_loads.append(pltpu.make_async_copy(w, w_v.at[t], load_sem.at[1 + t]))
-    weight_loads.append(pltpu.make_async_copy(w_out_in, w_out_v, load_sem.at[6]))
-    small_loads = [
-        pltpu.make_async_copy(valid_row, valid_v, load_sem.at[7]),
-        pltpu.make_async_copy(valid_s_in, valid_s, load_sem.at[8]),
-        pltpu.make_async_copy(gain_in, gain_s, load_sem.at[9]),
-        pltpu.make_async_copy(bias_in, bias_s, load_sem.at[10]),
-        pltpu.make_async_copy(out_gain_in, out_gain_s, load_sem.at[11]),
-        pltpu.make_async_copy(out_bias_in, out_bias_s, load_sem.at[12]),
+    own_rows = pltpu.make_async_copy(pair.at[:, z_hi], xin.at[pl.ds(z_hi * 32, 32)], load_sem.at[0])
+    weight_loads = [
+        pltpu.make_async_copy(w.at[x], w_all.at[t, z_hi, x], load_sem.at[1 + t])
+        for t, w in enumerate((w0, w1, w2, w3, w4))
     ]
-    for copy in weight_loads + small_loads:
+    out_loads = [
+        pltpu.make_async_copy(w_out_in, w_out_v, load_sem.at[6]),
+        pltpu.make_async_copy(out_gain_in, out_gain_s, load_sem.at[7]),
+        pltpu.make_async_copy(out_bias_in, out_bias_s, load_sem.at[8]),
+    ]
+    in_loads = [
+        pltpu.make_async_copy(valid_row, valid_v, load_sem.at[9]),
+        pltpu.make_async_copy(valid_s_in, valid_s, load_sem.at[10]),
+        pltpu.make_async_copy(gain_in, gain_s, load_sem.at[11]),
+        pltpu.make_async_copy(bias_in, bias_s, load_sem.at[12]),
+    ]
+    for copy in weight_loads + out_loads + in_loads + [own_rows]:
         copy.start()
-
-    pl.semaphore_wait(barrier, 23)
-
-    for t in (2, 1, 3):
-        ph = hi_peer(t)
-        remote(
-            pair.at[:, :, ph], xin.at[pl.ds(z_hi * 2, 2)], send_sem.at[0], recv_sem.at[0], at_hi(ph)
-        ).start()
-
-    for copy in weight_loads + small_loads:
+    for copy in weight_loads + out_loads:
         copy.wait()
-    pick = one_hot((16, 32), x * 8)
-    for t in range(5):
-        turned = lax.dot_general(pick, w_v[t], NT, preferred_element_type=F32)
-        w_all[t, z_hi, x] = turned[0:8].astype(BF16)
     lane = lax.broadcasted_iota(jnp.int32, (8, 128), 1)
     line = lax.broadcasted_iota(jnp.int32, (8, 128), 0)
 
@@ -160,59 +149,73 @@
         return jnp.where(lane == z_hi * 32 + i, value, held)
 
     edge[...] = lax.fori_loop(0, 32, put_edge, jnp.zeros((8, 128), F32))
-    for t in (1, 2, 3):
-        ph = hi_peer(t)
-        remote(
-            w_all.at[:, z_hi, x], w_all.at[:, z_hi, x], send_sem.at[1], recv_sem.at[1], at_hi(ph)
-        ).start()
-        remote(edge, edge_all.at[z_hi], send_sem.at[2], recv_sem.at[2], at_hi(ph)).start()
     edge_all[z_hi] = edge[...]
     w_out_t[...] = lax.dot_general(
         one_hot((128, 128), 0), w_out_v[...], NT, preferred_element_type=F32
     ).astype(BF16)
+
+    pl.semaphore_wait(barrier, 23)
+
+    for t in (2, 1, 3):
+        ph = hi_peer(t)
+        remote(
+            w_all.at[:, z_hi, x], w_all.at[:, z_hi, x], send_sem.at[1], recv_sem.at[1], at_hi(ph)
+        ).start()
+    for t in (2, 1, 3):
+        ph = hi_peer(t)
+        remote(
+            pair.at[:, ph], xin.at[pl.ds(z_hi * 32, 32)], send_sem.at[0], recv_sem.at[0], at_hi(ph)
+        ).start()
+    for t in (2, 1, 3):
+        ph = hi_peer(t)
+        remote(edge, edge_all.at[z_hi], send_sem.at[2], recv_sem.at[2], at_hi(ph)).start()
+    for copy in in_loads:
+        copy.wait()
     wait_bytes(w_all.at[:, 0, pl.ds(0, 3)], recv_sem.at[1])
-    for t in (1, 2, 3):
+    for t in (2, 1, 3):
         px = lax.rem(x + t, 4)
         remote(
             w_all.at[:, :, x], w_all.at[:, :, x], send_sem.at[3], recv_sem.at[3], at_xy(px, y)
         ).start()
-    wait_bytes(edge_all.at[pl.ds(0, 3)], recv_sem.at[2])
-    edge_sum = edge_all[0] + edge_all[1] + edge_all[2] + edge_all[3]
-    out_gain = jnp.transpose(jnp.broadcast_to(edge_sum[0:1], (128, 128)))
-    out_shift = jnp.transpose(jnp.broadcast_to(edge_sum[1:2], (128, 128)))
 
     own_rows.wait()
-    wait_bytes(xin.at[pl.ds(0, 6)], recv_sem.at[0])
+    wait_bytes(xin.at[pl.ds(0, 96)], recv_sem.at[0])
     centred(xin, wide, gain_s, bias_s)
 
     wait_bytes(w_all.at[:, :, pl.ds(0, 3)], recv_sem.at[3])
     col_valid = valid_v[pl.ds(x, 1), :].astype(F32)
     first_row = row * 32 + z_hi * 8
 
-    def project(step, _):
-        normed, masks = [], []
-        for member in range(2):
-            r = step * 2 + member
-            normed.append(wide[pl.ds(r, 128, stride=8), :].astype(BF16))
-            masks.append(col_valid * valid_s[first_row + r].astype(F32))
-        normed = jnp.concatenate(normed, axis=1)
-        mask = jnp.concatenate(masks, axis=1)
-
-        def linear(t):
-            return jnp.dot(rows_of(w_all[t]), normed, preferred_element_type=F32)
-
-        left = jax.nn.sigmoid(linear(0)) * linear(1) * mask
-        right = jax.nn.sigmoid(linear(2)) * linear(3) * mask
-        gate = jax.nn.sigmoid(linear(4)).astype(BF16).astype(F32)
+    def rows_at(step):
+        normed = [wide[pl.ds(step * 2 + member, 128, stride=8), :].astype(BF16) for member in range(2)]
+        return jnp.concatenate(normed, axis=1)
+
+    def linear(t, normed):
+        return jnp.dot(rows_of(w_all[t]), normed, preferred_element_type=F32)
+
+    def put_rows(ref, step, value):
         for member in range(2):
             at = pl.ds(pl.multiple_of((step * 2 + member) * 128, 128), 128)
-            lanes = slice(member * 128, member * 128 + 128)
-            left_f[at, :] = left[:, lanes]
-            right_f[at, :] = right[:, lanes]
-            gate_f[at, :] = gate[:, lanes]
-        return 0
-
-    lax.fori_loop(0, 4, project, 0)
+            ref[at, :] = value[:, member * 128 : member * 128 + 128]
+
+    def edges(first, ref):
+        def project(step, _):
+            normed = rows_at(step)
+            masks = [
+                col_valid * valid_s[first_row + step * 2 + member].astype(F32) for member in range(2)
+            ]
+            value = jax.nn.sigmoid(linear(first, normed)) * linear(first + 1, normed)
+            put_rows(ref, step, value * jnp.concatenate(masks, axis=1))
+            return 0
+
+        lax.fori_loop(0, 4, project, 0)
+
+    def gates(step, _):
+        value = jax.nn.sigmoid(linear(4, rows_at(step)))
+        put_rows(gate_f, step, value.astype(BF16).astype(F32))
+        return 0
+
+    edges(2, right_f)
     by_channel(right_f, right_send)
 
     def send_right(t, _):
@@ -229,6 +232,7 @@
 
     lax.fori_loop(1, 16, send_right, 0)
     own_right = own(right_send.at[:, xy], right_mid.at[xy], 0)
+    edges(0, left_f)
     by_channel(left_f, left_send)
 
     def send_left(t, _):
@@ -271,6 +275,8 @@
 
     lax.fori_loop(1, 16, pass_left, 0)
     own_left = own(left_mid.at[:, xy], left_all.at[xy], 3)
+
+    lax.fori_loop(0, 4, gates, 0)
 
     own_right.wait()
 
@@ -289,6 +295,8 @@
     own_left.wait()
     wait_bytes(left_all.at[pl.ds(0, 15)], recv_sem.at[7])
     wait_bytes(right_all.at[:, pl.ds(0, 8)], sibling_recv)
+
+    wait_bytes(edge_all.at[pl.ds(0, 3)], recv_sem.at[2])
 
     for part in range(4):
         total = jnp.zeros((256, 128), F32)
@@ -302,28 +310,25 @@
             )
 
     def send_mixed(t, _):
-        pz = z_peer(t)
-        remote(
-            mixed_send.at[pz], mixed_mid.at[z], send_sem.at[8], recv_sem.at[8], at_z(pz)
-        ).start()
-        return 0
-
-    lax.fori_loop(1, 8, send_mixed, 0)
-    own(mixed_send.at[z], mixed_mid.at[z], 4).wait()
-    wait_bytes(mixed_mid.at[pl.ds(0, 7)], recv_sem.at[8])
-
-    def pass_mixed(t, _):
-        px, py = xy_peer(t)
-        remote(
-            mixed_mid.at[:, py * 4 + px], mixed_all.at[:, xy], send_sem.at[9], recv_sem.at[9], at_xy(px, py)
-        ).start()
-        return 0
-
-    lax.fori_loop(1, 16, pass_mixed, 0)
-    own(mixed_mid.at[:, xy], mixed_all.at[:, xy], 5).wait()
-    wait_bytes(mixed_all.at[:, pl.ds(0, 15)], recv_sem.at[9])
+        i, q = t // 16, t % 16
+        away = lax.rem(4 + (1 - 2 * (i % 2)) * ((i + 1) // 2) + 8, 8)
+        pz = lax.rem(z + away, 8)
+        px, py = lax.rem(x + 2 + q % 4, 4), lax.rem(y + 2 + q // 4, 4)
+        remote(
+            mixed_send.at[pz, py * 4 + px], mixed_all.at[z * 16 + xy], send_sem.at[8], recv_sem.at[8],
+            device_at(px, py, pz, core),
+        ).start()
+        return 0
+
+    lax.fori_loop(0, 122, send_mixed, 0)
+    lax.fori_loop(123, 128, send_mixed, 0)
+    own(mixed_send.at[z, xy], mixed_all.at[z * 16 + xy], 4).wait()
+    wait_bytes(mixed_all.at[pl.ds(0, 127)], recv_sem.at[8])
 
     centred(mixed_all, wide)
+    edge_sum = edge_all[0] + edge_all[1] + edge_all[2] + edge_all[3]
+    out_gain = jnp.transpose(jnp.broadcast_to(edge_sum[0:1], (128, 128)))
+    out_shift = jnp.transpose(jnp.broadcast_to(edge_sum[1:2], (128, 128)))
 
     def finish(step, _):
         normed = []
@@ -350,7 +355,7 @@
     own(out_send.at[pl.ds(z_hi * 2, 2)], out.at[:, :, z_hi], 6).wait()
     wait_bytes(out.at[:, :, pl.ds(0, 3)], recv_sem.at[10])
 
-    wait_bytes(xin.at[pl.ds(0, 6)], send_sem.at[0])
+    wait_bytes(xin.at[pl.ds(0, 96)], send_sem.at[0])
     wait_bytes(w_all.at[:, 0, pl.ds(0, 3)], send_sem.at[1])
     wait_bytes(edge_all.at[pl.ds(0, 3)], send_sem.at[2])
     wait_bytes(w_all.at[:, :, pl.ds(0, 3)], send_sem.at[3])
@@ -358,8 +363,7 @@
     wait_bytes(left_mid.at[pl.ds(0, 7)], send_sem.at[5])
     wait_bytes(right_mid.at[:, pl.ds(0, 7)], send_sem.at[6])
     wait_bytes(left_all.at[pl.ds(0, 15)], send_sem.at[7])
-    wait_bytes(mixed_mid.at[pl.ds(0, 7)], send_sem.at[8])
-    wait_bytes(mixed_all.at[:, pl.ds(0, 15)], send_sem.at[9])
+    wait_bytes(mixed_all.at[pl.ds(0, 127)], send_sem.at[8])
     wait_bytes(out.at[:, :, pl.ds(0, 3)], send_sem.at[10])
     wait_bytes(right_all.at[:, pl.ds(0, 8)], sibling_send)
 
@@ -378,7 +382,7 @@
     out_bias,
     w_out,
 ):
-    any_spec = pl.BlockSpec(memory_space=pl.ANY)
+    any_spec = pl.BlockSpec(memory_space=pltpu.HBM)
     result = pl.pallas_call(
         kernel,
         name="triangle",
@@ -386,15 +390,14 @@
         in_specs=[any_spec] * 13,
         out_specs=any_spec,
         scratch_shapes=[
-            pltpu.VMEM((8, 16, 8, 128), BF16),
+            pltpu.VMEM((128, 8, 128), BF16),
             pltpu.VMEM((4, 128), jnp.int32),
             pltpu.SMEM((512,), jnp.int32),
             pltpu.SMEM((128,), F32),
             pltpu.SMEM((128,), F32),
             pltpu.SMEM((32,), F32),
             pltpu.SMEM((32,), F32),
-            pltpu.VMEM((5, 128, 32), BF16),
-            pltpu.VMEM((128, 128), BF16),
+                pltpu.VMEM((128, 128), BF16),
             pltpu.VMEM((5, 4, 4, 8, 128), BF16),
             pltpu.VMEM((128, 128), BF16),
             pltpu.VMEM((8, 128), F32),
@@ -410,8 +413,7 @@
             pltpu.VMEM((16, 8, 8, 128), BF16),
             pltpu.VMEM((16, 16, 8, 128), BF16),
             pltpu.VMEM((8, 16, 8, 128), BF16),
-            pltpu.VMEM((8, 16, 8, 128), BF16),
-            pltpu.VMEM((8, 16, 8, 128), BF16),
+            pltpu.VMEM((128, 8, 128), BF16),
             pltpu.VMEM((8, 16, 8, 128), BF16),
             pltpu.SemaphoreType.DMA((13,)),
             pltpu.SemaphoreType.DMA((11,)),
@@ -422,19 +424,19 @@
             pltpu.SemaphoreType.DMA,
         ],
         compiler_params=pltpu.CompilerParams(
-            collective_id=0, has_side_effects=True, vmem_limit_bytes=32 << 20
+            collective_id=0, has_side_effects=True, vmem_limit_bytes=62 << 20
         ),
     )(
-        pair.reshape(2, 16, 4, 8, 128),
+        pair.reshape(32, 4, 8, 128),
         token_valid.reshape(4, 128),
         token_valid,
         ln_gain,
         ln_bias,
-        w_agate,
-        w_aproj,
-        w_bgate,
-        w_bproj,
-        w_gate,
+        w_agate.T.reshape(4, 8, 128),
+        w_aproj.T.reshape(4, 8, 128),
+        w_bgate.T.reshape(4, 8, 128),
+        w_bproj.T.reshape(4, 8, 128),
+        w_gate.T.reshape(4, 8, 128),
         out_gain,
         out_bias,
         w_out,

time: 70.8 us -> 60.4 us (0.85)
  Pallas kernels: 65.2 us -> 58.6 us
  local copies, waits for them, and re-layouts: 5.27 us -> 1.67 us
    pallas_call x1, Pallas kernels: 65.2 us -> 58.6 us  [on_device(): pl.pallas_call(kernel, name='triangle', out_shape=jax.ShapeDtypeStruct((2...]
    unnamed x28 -> x1, local copies, waits for them, and re-layouts: 5.27 us -> 1.67 us
where the time goes in v2:
time: 60.4 us; the launch traced here: 60.2 us
  Pallas kernels  58.6 us (97%)
  local copies, waits for them, and re-layouts  1.67 us (3%)
    pallas_call x1, Pallas kernels, on_device(): pl.pallas_call(kernel, name='triangle', out_shape=jax.ShapeDtypeStruct((2...  58.6 us
    unnamed x1, local copies, waits for them, and re-layouts  1.67 us

profile of v2, /device:TPU:1, one launch (start us, length us, event | category | flops | bytes accessed | tf_op | source)
XLA Modules:
  0.0 60.2 jit_solution(6864503456630688488)
XLA Ops:
  0.0 58.6 %triangle.1 = bf16[2,16,4,8,128]{4,3,2,1,0:T(8,128)(2,1)} custom-call(bf16[32,4,8,128]{3,2,1,0:T(8,128)(2,1)} %bitcast.19, s32[4,128]{1,0:T(4,128)} %bitcast.25, s32[512]{0:T(512)} %valid_s_in.1, f32[128]{0:T(128)} %gain_in.1, f32[128]{0:T(128)} %bias_in.1, bf16[4,8,128]{2,1,0:T(8,128)(2,1)} %bitcast.20, bf16[4,8,128]{2,1,0:T(8,128)(2,1)} %bitcast.21, ...), custom_call_target="tpu_custom_call" | custom-call | tf_op jit(solution)/shard_map/triangle/pallas_call | solution.py:386
  58.6 1.7 %copy.14 = bf16[32,32,128]{2,1,0:T(8,128)(2,1)} copy(bf16[32,32,128]{2,1,0:T(8,128)(2,1)} %bitcast.18) | data formatting | bytes 524288

commit v3 on v2

v3 whole, which is shorter than its diff:
```python
import jax
import jax.numpy as jnp
from jax import lax
from jax.experimental import pallas as pl
from jax.experimental.pallas import tpu as pltpu
from jax.sharding import PartitionSpec as P

EPSILON = 1e-05
MESH = pl.DeviceIdType.MESH
F32 = jnp.float32
BF16 = jnp.bfloat16
NT = (((1,), (1,)), ((), ()))
Z_AWAY = (4, 3, 5, 2, 6, 1, 7, 0)
MIRROR = (0, 2, 1, 4, 3, 6, 5, 7)
GROUPS = ((0, 1, 2), (3, 4, 5, 6, 7))


def device_at(x, y, z, core):
    return ((y * 2 + z % 2) * 2 + core, x, z // 2)


def wait_bytes(ref, sem):
    pltpu.make_async_copy(ref, ref, sem).wait()


def remote(src, dst, send_sem, recv_sem, device):
    return pltpu.make_async_remote_copy(
        src, dst, send_sem, recv_sem, device_id=device, device_id_type=MESH
    )


def rows_of(block):
    return block.astype(F32).reshape(-1, 128).astype(BF16)


def one_hot(shape, offset):
    first = lax.broadcasted_iota(jnp.int32, shape, 0)
    second = lax.broadcasted_iota(jnp.int32, shape, 1)
    return (second == first + offset).astype(F32).astype(BF16)


def centred(blocks, scratch, gain=None, shift=None):
    def add(step, total):
        part = blocks[pl.ds(step * 16, 16)].astype(F32)
        return total + jnp.sum(part, axis=0)

    centre = lax.fori_loop(0, 8, add, jnp.zeros((8, 128), F32)) * (1.0 / 128)

    def add_square(step, total):
        part = blocks[pl.ds(step * 16, 16)].astype(F32) - centre
        return total + jnp.sum(part * part, axis=0)

    spread = lax.fori_loop(0, 8, add_square, jnp.zeros((8, 128), F32)) * (1.0 / 128)
    scale = lax.rsqrt(spread + EPSILON)

    def put(step, _):
        for member in range(16):
            c = step * 16 + member
            value = (blocks[c].astype(F32) - centre) * scale
            if gain is not None:
                value = value * gain[c] + shift[c]
            scratch[pl.ds(pl.multiple_of(c * 8, 8), 8), :] = value
        return 0

    lax.fori_loop(0, 8, put, 0)


def by_channel(scratch, out, first=0, count=8):
    def put(step, _):
        for member in range(16):
            out[step, member] = scratch[pl.ds(step * 16 + member, 8, stride=128), :].astype(BF16)
        return 0

    lax.fori_loop(first, first + count, put, 0)


def kernel(
    pair, valid_row, valid_s_in, gain_in, bias_in, w0, w1, w2, w3, w4, out_gain_in, out_bias_in, w_out_in,
    out,
    xin, valid_v, valid_s, gain_s, bias_s, out_gain_s, out_bias_s, w_out_v, w_all, w_out_t,
    edge, edge_all,
    wide, left_f, right_f, gate_f,
    left_send, left_all, right_send, right_all, mixed_send, mixed_all, out_send,
    load_sem, send_sem, recv_sem, own_sem, sibling_send, left_recv, right_recv, sibling_recv, plane_sem,
):
    row, x, z_hi = lax.axis_index("row"), lax.axis_index("col"), lax.axis_index("chan")
    core, z_lo, y = row % 2, (row // 2) % 2, row // 4
    z = z_hi * 2 + z_lo
    xy = y * 4 + x

    def hi_peer(t):
        return (z_hi + t) % 4

    def at_hi(ph):
        return (row, x, ph)

    sibling = device_at(x, y, z, 1 - core)
    z_peers = [(z + away) % 8 for away in Z_AWAY]

    barrier = pltpu.get_barrier_semaphore()
    for pz in z_peers[:7]:
        pl.semaphore_signal(
            barrier, inc=1, device_id=device_at(x, y, pz, core), device_id_type=MESH
        )

    def greet_xy(t, _):
        pl.semaphore_signal(
            barrier,
            inc=1,
            device_id=device_at((x + t % 4) % 4, (y + t // 4) % 4, z, core),
            device_id_type=MESH,
        )
        return 0

    lax.fori_loop(1, 16, greet_xy, 0)
    pl.semaphore_signal(barrier, inc=1, device_id=sibling, device_id_type=MESH)

    half = pl.ds(core * 2, 2)
    own_rows = pltpu.make_async_copy(pair.at[:, z_hi], xin.at[pl.ds(z_hi * 32, 32)], load_sem.at[0])
    weight_loads = [
        pltpu.make_async_copy(w.at[x], w_all.at[t, z_hi, x], load_sem.at[1 + t])
        for t, w in enumerate((w0, w1, w2))
    ] + [
        pltpu.make_async_copy(w.at[half], w_all.at[3 + t, z_hi, half], load_sem.at[4 + t])
        for t, w in enumerate((w3, w4))
    ]
    out_loads = [
        pltpu.make_async_copy(w_out_in, w_out_v, load_sem.at[6]),
        pltpu.make_async_copy(out_gain_in, out_gain_s, load_sem.at[7]),
        pltpu.make_async_copy(out_bias_in, out_bias_s, load_sem.at[8]),
    ]
    in_loads = [
        pltpu.make_async_copy(valid_row, valid_v, load_sem.at[9]),
        pltpu.make_async_copy(valid_s_in, valid_s, load_sem.at[10]),
        pltpu.make_async_copy(gain_in, gain_s, load_sem.at[11]),
        pltpu.make_async_copy(bias_in, bias_s, load_sem.at[12]),
    ]
    for copy in weight_loads + out_loads + in_loads + [own_rows]:
        copy.start()
    for copy in weight_loads + out_loads:
        copy.wait()
    lane = lax.broadcasted_iota(jnp.int32, (8, 128), 1)
    line = lax.broadcasted_iota(jnp.int32, (8, 128), 0)

    def put_edge(i, held):
        value = jnp.where(line == 0, out_gain_s[i], out_bias_s[i])
        return jnp.where(lane == z_hi * 32 + i, value, held)

    edge[...] = lax.fori_loop(0, 32, put_edge, jnp.zeros((8, 128), F32))
    edge_all[z_hi] = edge[...]
    w_out_t[...] = lax.dot_general(
        one_hot((128, 128), 0), w_out_v[...], NT, preferred_element_type=F32
    ).astype(BF16)

    pl.semaphore_wait(barrier, 23)

    right_weights = w_all.at[pl.ds(3, 2), z_hi, half]
    left_weights = w_all.at[pl.ds(0, 3), z_hi, x]
    for t in (2, 1, 3):
        ph = hi_peer(t)
        remote(right_weights, right_weights, send_sem.at[1], recv_sem.at[1], at_hi(ph)).start()
    for t in (2, 1, 3):
        ph = hi_peer(t)
        remote(left_weights, left_weights, send_sem.at[9], recv_sem.at[9], at_hi(ph)).start()
    for t in (2, 1, 3):
        ph = hi_peer(t)
        remote(
            pair.at[:, ph], xin.at[pl.ds(z_hi * 32, 32)], send_sem.at[0], recv_sem.at[0], at_hi(ph)
        ).start()
    for pz in z_peers[:7]:
        pl.semaphore_signal(
            plane_sem, inc=1, device_id=device_at(x, y, pz, core), device_id_type=MESH
        )
    for t in (2, 1, 3):
        ph = hi_peer(t)
        remote(edge, edge_all.at[z_hi], send_sem.at[2], recv_sem.at[2], at_hi(ph)).start()
    for copy in in_loads:
        copy.wait()
    wait_bytes(w_all.at[pl.ds(3, 2), pl.ds(0, 3), pl.ds(0, 2)], recv_sem.at[1])
    right_weights = w_all.at[pl.ds(3, 2), :, half]
    remote(right_weights, right_weights, send_sem.at[4], recv_sem.at[4], sibling).start()
    wait_bytes(w_all.at[pl.ds(0, 3), pl.ds(0, 3), 0], recv_sem.at[9])
    left_weights = w_all.at[pl.ds(0, 3), :, x]
    for t in (2, 1, 3):
        remote(
            left_weights, left_weights, send_sem.at[3], recv_sem.at[3],
            device_at((x + t) % 4, y, z, core),
        ).start()

    own_rows.wait()
    wait_bytes(xin.at[pl.ds(0, 96)], recv_sem.at[0])
    centred(xin, wide, gain_s, bias_s)

    wait_bytes(w_all.at[pl.ds(3, 2), :, pl.ds(0, 2)], recv_sem.at[4])
    col_valid = valid_v[pl.ds(x, 1), :].astype(F32)
    first_row = row * 32 + z_hi * 8

    def rows_at(step):
        normed = [wide[pl.ds(step * 2 + member, 128, stride=8), :].astype(BF16) for member in range(2)]
        return jnp.concatenate(normed, axis=1)

    def linear(t, normed):
        return jnp.dot(rows_of(w_all[t]), normed, preferred_element_type=F32)

    def put_rows(ref, step, value):
        for member in range(2):
            at = pl.ds(pl.multiple_of((step * 2 + member) * 128, 128), 128)
            ref[at, :] = value[:, member * 128 : member * 128 + 128]

    def edges(first, ref):
        def project(step, _):
            normed = rows_at(step)
            masks = [
                col_valid * valid_s[first_row + step * 2 + member].astype(F32) for member in range(2)
            ]
            value = jax.nn.sigmoid(linear(first, normed)) * linear(first + 1, normed)
            put_rows(ref, step, value * jnp.concatenate(masks, axis=1))
            return 0

        lax.fori_loop(0, 4, project, 0)

    def gates(step, _):
        value = jax.nn.sigmoid(linear(2, rows_at(step)))
        put_rows(gate_f, step, value.astype(BF16).astype(F32))
        return 0

    def own(src, dst, i):
        copy = pltpu.make_async_copy(src, dst, own_sem.at[i])
        copy.start()
        return copy

    def xy_peer(k):
        px, py = (x + 2 + k % 4) % 4, (y + 2 + k // 4) % 4
        return px, py, py * 4 + px

    def to_all(start, places):
        def plane(k, _):
            px, py, pxy = xy_peer(k)
            for i in places:
                if i < 7:
                    start(i, px, py, pxy)
                else:
                    pl.when(k != 10)(lambda: start(7, px, py, pxy))
            return 0

        lax.fori_loop(0, 16, plane, 0)

    edges(3, right_f)
    by_channel(right_f, right_send)
    pl.semaphore_wait(plane_sem, 7)

    def slot(pz, pcore):
        return (pz % 2) * 8 + pcore * 4 + pz // 2

    mine = slot(z, core)

    def send_right(i, px, py, pxy):
        remote(
            right_send.at[z_peers[i], pxy], right_all.at[xy, mine],
            send_sem.at[5], right_recv.at[MIRROR[i]], device_at(px, py, z_peers[i], core),
        ).start()

    to_all(send_right, range(8))
    own_right = own(right_send.at[z, xy], right_all.at[xy, mine], 0)

    wait_bytes(w_all.at[pl.ds(0, 3), :, pl.ds(0, 3)], recv_sem.at[3])
    edges(0, left_f)
    by_channel(left_f, left_send)

    def send_left(i, px, py, pxy):
        remote(
            left_send.at[z_peers[i], pxy], left_all.at[x, MIRROR[i], y],
            send_sem.at[6], left_recv.at[MIRROR[i]], device_at(px, py, z_peers[i], core),
        ).start()

    to_all(send_left, range(8))
    own_left = own(left_send.at[z, xy], left_all.at[x, 7, y], 1)
    lax.fori_loop(0, 4, gates, 0)

    for i in range(8):
        if i == 7:
            own_right.wait()
            wait_bytes(right_all.at[pl.ds(0, 15), 0], right_recv.at[7])
        else:
            wait_bytes(right_all.at[:, 0], right_recv.at[i])
        part = right_all.at[:, slot(z_peers[i], core)]
        remote(part, part, sibling_send, sibling_recv, sibling).start()
    wait_bytes(right_all.at[:, pl.ds(0, 8)], sibling_recv)
    wait_bytes(edge_all.at[pl.ds(0, 3)], recv_sem.at[2])

    def send_mixed(i, px, py, pxy):
        remote(
            mixed_send.at[i, pxy], mixed_all.at[z * 16 + xy], send_sem.at[7], recv_sem.at[7],
            device_at(px, py, z_peers[i], core),
        ).start()

    for group in GROUPS:
        first, count = group[0], len(group)
        for i in group:
            if i == 7:
                own_left.wait()
                wait_bytes(right_all.at[pl.ds(0, 15), 0], left_recv.at[7])
            else:
                wait_bytes(left_all.at[:, 0], left_recv.at[i])
        left = jnp.concatenate(
            [rows_of(left_all[step, pl.ds(first, count)]) for step in range(4)], axis=1
        )
        for part in range(4):
            right = jnp.concatenate([rows_of(right_all[part * 4 + step]) for step in range(4)], axis=1)
            total = lax.dot_general(left, right, NT, preferred_element_type=F32)
            total = total.reshape(count, 4, 8, 128).astype(BF16)
            for py in range(4):
                mixed_send[pl.ds(first, count), py * 4 + part] = total[:, py]
        to_all(send_mixed, group)
    own(mixed_send.at[7, xy], mixed_all.at[z * 16 + xy], 2).wait()
    wait_bytes(mixed_all.at[pl.ds(0, 127)], recv_sem.at[7])

    centred(mixed_all, wide)
    edge_sum = edge_all[0] + edge_all[1] + edge_all[2] + edge_all[3]
    out_gain = jnp.transpose(jnp.broadcast_to(edge_sum[0:1], (128, 128)))
    out_shift = jnp.transpose(jnp.broadcast_to(edge_sum[1:2], (128, 128)))

    def finish(step, _):
        normed = []
        for member in range(2):
            r = step * 2 + member
            value = wide[pl.ds(r, 128, stride=8), :] * out_gain + out_shift
            normed.append(value.astype(BF16))
        projected = jnp.dot(
            w_out_t[...], jnp.concatenate(normed, axis=1), preferred_element_type=F32
        )
        for member in range(2):
            at = pl.ds(pl.multiple_of((step * 2 + member) * 128, 128), 128)
            left_f[at, :] = gate_f[at, :] * projected[:, member * 128 : member * 128 + 128]
        return 0

    lax.fori_loop(0, 4, finish, 0)

    for t in (2, 1, 3, 0):
        ph = hi_peer(t)
        part = out_send.at[pl.ds(ph * 2, 2)]
        by_channel(left_f, out_send, ph * 2, 2)
        if t:
            remote(part, out.at[:, :, z_hi], send_sem.at[8], recv_sem.at[8], at_hi(ph)).start()
        else:
            own(part, out.at[:, :, z_hi], 3).wait()
    wait_bytes(out.at[:, :, pl.ds(0, 3)], recv_sem.at[8])

    wait_bytes(xin.at[pl.ds(0, 96)], send_sem.at[0])
    wait_bytes(w_all.at[pl.ds(3, 2), pl.ds(0, 3), pl.ds(0, 2)], send_sem.at[1])
    wait_bytes(edge_all.at[pl.ds(0, 3)], send_sem.at[2])
    wait_bytes(w_all.at[pl.ds(0, 3), :, pl.ds(0, 3)], send_sem.at[3])
    wait_bytes(w_all.at[pl.ds(3, 2), :, pl.ds(0, 2)], send_sem.at[4])
    wait_bytes(mixed_all.at[pl.ds(0, 127)], send_sem.at[5])
    wait_bytes(mixed_all.at[pl.ds(0, 127)], send_sem.at[6])
    wait_bytes(mixed_all.at[pl.ds(0, 127)], send_sem.at[7])
    wait_bytes(out.at[:, :, pl.ds(0, 3)], send_sem.at[8])
    wait_bytes(w_all.at[pl.ds(0, 3), pl.ds(0, 3), 0], send_sem.at[9])
    wait_bytes(right_all.at[:, pl.ds(0, 8)], sibling_send)


def on_device(
    pair,
    token_valid,
    ln_gain,
    ln_bias,
    w_agate,
    w_aproj,
    w_bgate,
    w_bproj,
    w_gate,
    out_gain,
    out_bias,
    w_out,
):
    any_spec = pl.BlockSpec(memory_space=pltpu.HBM)
    operands = [
        pltpu.with_memory_space_constraint(array, pltpu.HBM)
        for array in (
            pair.reshape(32, 4, 8, 128),
            token_valid.reshape(4, 128),
            token_valid,
            ln_gain,
            ln_bias,
            w_agate.T.reshape(4, 8, 128),
            w_aproj.T.reshape(4, 8, 128),
            w_gate.T.reshape(4, 8, 128),
            w_bgate.T.reshape(4, 8, 128),
            w_bproj.T.reshape(4, 8, 128),
            out_gain,
            out_bias,
            w_out,
        )
    ]
    result = pl.pallas_call(
        kernel,
        name="triangle",
        out_shape=pltpu.VMEM((2, 16, 4, 8, 128), BF16),
        in_specs=[any_spec] * 13,
        out_specs=pl.BlockSpec(memory_space=pl.ANY),
        scratch_shapes=[
            pltpu.VMEM((128, 8, 128), BF16),
            pltpu.VMEM((4, 128), jnp.int32),
            pltpu.SMEM((512,), jnp.int32),
            pltpu.SMEM((128,), F32),
            pltpu.SMEM((128,), F32),
            pltpu.SMEM((32,), F32),
            pltpu.SMEM((32,), F32),
                pltpu.VMEM((128, 128), BF16),
            pltpu.VMEM((5, 4, 4, 8, 128), BF16),
            pltpu.VMEM((128, 128), BF16),
            pltpu.VMEM((8, 128), F32),
            pltpu.VMEM((4, 8, 128), F32),
            pltpu.VMEM((1024, 128), F32),
            pltpu.VMEM((1024, 128), F32),
            pltpu.VMEM((1024, 128), F32),
            pltpu.VMEM((1024, 128), F32),
            pltpu.VMEM((8, 16, 8, 128), BF16),
            pltpu.VMEM((4, 8, 4, 8, 128), BF16),
            pltpu.VMEM((8, 16, 8, 128), BF16),
            pltpu.VMEM((16, 16, 8, 128), BF16),
            pltpu.VMEM((8, 16, 8, 128), BF16),
            pltpu.VMEM((128, 8, 128), BF16),
            pltpu.VMEM((8, 16, 8, 128), BF16),
            pltpu.SemaphoreType.DMA((13,)),
            pltpu.SemaphoreType.DMA((10,)),
            pltpu.SemaphoreType.DMA((10,)),
            pltpu.SemaphoreType.DMA((4,)),
            pltpu.SemaphoreType.DMA,
            pltpu.SemaphoreType.DMA((8,)),
            pltpu.SemaphoreType.DMA((8,)),
            pltpu.SemaphoreType.DMA,
            pltpu.SemaphoreType.REGULAR,
        ],
        compiler_params=pltpu.CompilerParams(
            collective_id=0, has_side_effects=True, vmem_limit_bytes=32 << 20
        ),
    )(*operands)
    return result.reshape(32, 32, 128)


def solution(mesh):
    return jax.shard_map(
        on_device,
        mesh=mesh,
        in_specs=(
            P("chan", "row", "col"),
            P(),
            P(),
            P(),
            P(None, "chan"),
            P(None, "chan"),
            P(None, "chan"),
            P(None, "chan"),
            P(None, "chan"),
            P("chan"),
            P("chan"),
            P(),
        ),
        out_specs=P("chan", "row", "col"),
        check_vma=False,
    )
```

time: 60.4 us -> 55.5 us (0.919); the launches traced: 60.2 us -> 54.5 us
  Pallas kernels: 58.6 us -> 53.8 us
  local copies, waits for them, and re-layouts: 1.67 us -> 0.71 us
    pallas_call x1, Pallas kernels: 58.6 us -> 53.8 us  [on_device(): pl.pallas_call(kernel, name='triangle', out_shape=pltpu.VMEM((2, 16, 4, 8...]
    unnamed x1, local copies, waits for them, and re-layouts: 1.67 us -> 0.71 us
where the time goes in v3:
time: 55.5 us; the launch traced here: 54.5 us
  Pallas kernels  53.8 us (97%)
  local copies, waits for them, and re-layouts  0.71 us (1%)
    pallas_call x1, Pallas kernels, on_device(): pl.pallas_call(kernel, name='triangle', out_shape=pltpu.VMEM((2, 16, 4, 8...  53.8 us

profile of v3, /device:TPU:1, one launch (start us, length us, event | category | flops | bytes accessed | tf_op | source)
XLA Modules:
  0.0 54.5 jit_solution(2059623733552788378)
XLA Ops:
  0.0 53.8 %triangle.1 = bf16[2,16,4,8,128]{4,3,2,1,0:T(8,128)(2,1)S(1)} custom-call(bf16[32,4,8,128]{3,2,1,0:T(8,128)(2,1)} %bitcast.19, s32[4,128]{1,0:T(4,128)} %bitcast.25, s32[512]{0:T(512)} %valid_s_in.1, f32[128]{0:T(128)} %gain_in.1, f32[128]{0:T(128)} %bias_in.1, bf16[4,8,128]{2,1,0:T(8,128)(2,1)} %bitcast.20, bf16[4,8,128]{2,1,0:T(8,128)(2,1)} %bitcast.21, ...), custom_call_target="tpu_custom_call" | custom-call | tf_op jit(solution)/shard_map/triangle/pallas_call | solution.py:395
  53.8 0.7 %copy.14 = bf16[32,32,128]{2,1,0:T(8,128)(2,1)} copy(bf16[32,32,128]{2,1,0:T(8,128)(2,1)S(1)} %bitcast.18) | data formatting | bytes 524288

commit v4 on v3

--- a/solution.py
+++ b/solution.py
@@ -12,7 +12,7 @@
 NT = (((1,), (1,)), ((), ()))
 Z_AWAY = (4, 3, 5, 2, 6, 1, 7, 0)
 MIRROR = (0, 2, 1, 4, 3, 6, 5, 7)
-GROUPS = ((0, 1, 2), (3, 4, 5, 6, 7))
+GROUPS = ((0,1,2),(3,4),(5,6,7))
 
 
 def device_at(x, y, z, core):
@@ -217,7 +217,7 @@
             put_rows(ref, step, value * jnp.concatenate(masks, axis=1))
             return 0
 
-        lax.fori_loop(0, 4, project, 0)
+        lax.fori_loop(0, 4, project, 0, unroll=True)
 
     def gates(step, _):
         value = jax.nn.sigmoid(linear(2, rows_at(step)))
@@ -229,21 +229,19 @@
         copy.start()
         return copy
 
-    def xy_peer(k):
-        px, py = (x + 2 + k % 4) % 4, (y + 2 + k // 4) % 4
-        return px, py, py * 4 + px
-
     def to_all(start, places):
-        def plane(k, _):
-            px, py, pxy = xy_peer(k)
-            for i in places:
-                if i < 7:
-                    start(i, px, py, pxy)
-                else:
-                    pl.when(k != 10)(lambda: start(7, px, py, pxy))
-            return 0
-
-        lax.fori_loop(0, 16, plane, 0)
+        for i in places:
+            def line(j, _):
+                py = (y + 2 + j) % 4
+                for m in range(4):
+                    px = (x + 2 + m) % 4
+                    if i < 7 or m != 2:
+                        start(i, px, py, py * 4 + px)
+                    else:
+                        pl.when(j != 2)(lambda: start(i, px, py, py * 4 + px))
+                return 0
+
+            lax.fori_loop(0, 4, line, 0)
 
     edges(3, right_f)
     by_channel(right_f, right_send)
@@ -275,7 +273,7 @@
 
     to_all(send_left, range(8))
     own_left = own(left_send.at[z, xy], left_all.at[x, 7, y], 1)
-    lax.fori_loop(0, 4, gates, 0)
+    lax.fori_loop(0, 4, gates, 0, unroll=True)
 
     for i in range(8):
         if i == 7:
@@ -334,7 +332,7 @@
             left_f[at, :] = gate_f[at, :] * projected[:, member * 128 : member * 128 + 128]
         return 0
 
-    lax.fori_loop(0, 4, finish, 0)
+    lax.fori_loop(0, 4, finish, 0, unroll=True)
 
     for t in (2, 1, 3, 0):
         ph = hi_peer(t)

time: 55.5 us -> 52 us (0.937); the launches traced: 54.5 us -> 51.9 us
  Pallas kernels: 53.8 us -> 51.2 us
    pallas_call x1, Pallas kernels: 53.8 us -> 51.2 us  [on_device(): pl.pallas_call(kernel, name='triangle', out_shape=pltpu.VMEM((2, 16, 4, 8...]
where the time goes in v4:
time: 52 us; the launch traced here: 51.9 us
  Pallas kernels  51.2 us (98%)
  local copies, waits for them, and re-layouts  0.71 us (1%)
    pallas_call x1, Pallas kernels, on_device(): pl.pallas_call(kernel, name='triangle', out_shape=pltpu.VMEM((2, 16, 4, 8...  51.2 us

profile of v4, /device:TPU:1, one launch (start us, length us, event | category | flops | bytes accessed | tf_op | source)
XLA Modules:
  0.0 51.9 jit_solution(2952179463073352768)
XLA Ops:
  0.0 51.2 %triangle.1 = bf16[2,16,4,8,128]{4,3,2,1,0:T(8,128)(2,1)S(1)} custom-call(bf16[32,4,8,128]{3,2,1,0:T(8,128)(2,1)} %bitcast.19, s32[4,128]{1,0:T(4,128)} %bitcast.25, s32[512]{0:T(512)} %valid_s_in.1, f32[128]{0:T(128)} %gain_in.1, f32[128]{0:T(128)} %bias_in.1, bf16[4,8,128]{2,1,0:T(8,128)(2,1)} %bitcast.20, bf16[4,8,128]{2,1,0:T(8,128)(2,1)} %bitcast.21, ...), custom_call_target="tpu_custom_call" | custom-call | tf_op jit(solution)/shard_map/triangle/pallas_call | solution.py:393
  51.2 0.7 %copy.14 = bf16[32,32,128]{2,1,0:T(8,128)(2,1)} copy(bf16[32,32,128]{2,1,0:T(8,128)(2,1)S(1)} %bitcast.18) | data formatting | bytes 524288

commit v5 on v4

--- a/solution.py
+++ b/solution.py
@@ -12,7 +12,7 @@
 NT = (((1,), (1,)), ((), ()))
 Z_AWAY = (4, 3, 5, 2, 6, 1, 7, 0)
 MIRROR = (0, 2, 1, 4, 3, 6, 5, 7)
-GROUPS = ((0,1,2),(3,4),(5,6,7))
+GROUPS = ((0, 1, 2), (3, 4), (5, 6, 7))
 
 
 def device_at(x, y, z, core):
@@ -40,17 +40,19 @@
 
 
 def centred(blocks, scratch, gain=None, shift=None):
+    n = blocks.shape[1]
+
     def add(step, total):
         part = blocks[pl.ds(step * 16, 16)].astype(F32)
         return total + jnp.sum(part, axis=0)
 
-    centre = lax.fori_loop(0, 8, add, jnp.zeros((8, 128), F32)) * (1.0 / 128)
+    centre = lax.fori_loop(0, 8, add, jnp.zeros((n, 128), F32)) * (1.0 / 128)
 
     def add_square(step, total):
         part = blocks[pl.ds(step * 16, 16)].astype(F32) - centre
         return total + jnp.sum(part * part, axis=0)
 
-    spread = lax.fori_loop(0, 8, add_square, jnp.zeros((8, 128), F32)) * (1.0 / 128)
+    spread = lax.fori_loop(0, 8, add_square, jnp.zeros((n, 128), F32)) * (1.0 / 128)
     scale = lax.rsqrt(spread + EPSILON)
 
     def put(step, _):
@@ -59,16 +61,18 @@
             value = (blocks[c].astype(F32) - centre) * scale
             if gain is not None:
                 value = value * gain[c] + shift[c]
-            scratch[pl.ds(pl.multiple_of(c * 8, 8), 8), :] = value
+            scratch[pl.ds(pl.multiple_of(c * n, n), n), :] = value
         return 0
 
     lax.fori_loop(0, 8, put, 0)
 
 
-def by_channel(scratch, out, first=0, count=8):
+def by_channel(scratch, out, first=0, count=8, base=0):
+    n = out.shape[2]
+
     def put(step, _):
         for member in range(16):
-            out[step, member] = scratch[pl.ds(step * 16 + member, 8, stride=128), :].astype(BF16)
+            out[step, member] = scratch[pl.ds(base + step * 16 + member, n, stride=128), :].astype(BF16)
         return 0
 
     lax.fori_loop(first, first + count, put, 0)
@@ -81,7 +85,7 @@
     edge, edge_all,
     wide, left_f, right_f, gate_f,
     left_send, left_all, right_send, right_all, mixed_send, mixed_all, out_send,
-    load_sem, send_sem, recv_sem, own_sem, sibling_send, left_recv, right_recv, sibling_recv, plane_sem,
+    load_sem, send_sem, recv_sem, own_sem, sibling_send, left_recv, right_recv, sibling_recv, mixed_recv, out_sem, plane_sem,
 ):
     row, x, z_hi = lax.axis_index("row"), lax.axis_index("col"), lax.axis_index("chan")
     core, z_lo, y = row % 2, (row // 2) % 2, row // 4
@@ -89,13 +93,13 @@
     xy = y * 4 + x
 
     def hi_peer(t):
-        return (z_hi + t) % 4
+        return (z_hi + t + core * (4 - 2 * t)) % 4
 
     def at_hi(ph):
         return (row, x, ph)
 
     sibling = device_at(x, y, z, 1 - core)
-    z_peers = [(z + away) % 8 for away in Z_AWAY]
+    z_peers = [(z + away + core * (8 - 2 * away)) % 8 for away in Z_AWAY]
 
     barrier = pltpu.get_barrier_semaphore()
     for pz in z_peers[:7]:
@@ -229,12 +233,15 @@
         copy.start()
         return copy
 
-    def to_all(start, places):
+    def to_all(start, places, prepare=None):
         for i in places:
+            if prepare is not None:
+                prepare(z_peers[i])
+
             def line(j, _):
-                py = (y + 2 + j) % 4
+                py = (y + 2 + j + core * (4 - 2 * j)) % 4
                 for m in range(4):
-                    px = (x + 2 + m) % 4
+                    px = (x + 2 + m + core * (4 - 2 * m)) % 4
                     if i < 7 or m != 2:
                         start(i, px, py, py * 4 + px)
                     else:
@@ -244,7 +251,6 @@
             lax.fori_loop(0, 4, line, 0)
 
     edges(3, right_f)
-    by_channel(right_f, right_send)
     pl.semaphore_wait(plane_sem, 7)
 
     def slot(pz, pcore):
@@ -258,12 +264,11 @@
             send_sem.at[5], right_recv.at[MIRROR[i]], device_at(px, py, z_peers[i], core),
         ).start()
 
-    to_all(send_right, range(8))
+    to_all(send_right, range(8), lambda pz: by_channel(right_f, right_send, pz, 1))
     own_right = own(right_send.at[z, xy], right_all.at[xy, mine], 0)
 
     wait_bytes(w_all.at[pl.ds(0, 3), :, pl.ds(0, 3)], recv_sem.at[3])
     edges(0, left_f)
-    by_channel(left_f, left_send)
 
     def send_left(i, px, py, pxy):
         remote(
@@ -271,7 +276,7 @@
             send_sem.at[6], left_recv.at[MIRROR[i]], device_at(px, py, z_peers[i], core),
         ).start()
 
-    to_all(send_left, range(8))
+    to_all(send_left, range(8), lambda pz: by_channel(left_f, left_send, pz, 1))
     own_left = own(left_send.at[z, xy], left_all.at[x, 7, y], 1)
     lax.fori_loop(0, 4, gates, 0, unroll=True)
 
@@ -284,13 +289,15 @@
         part = right_all.at[:, slot(z_peers[i], core)]
         remote(part, part, sibling_send, sibling_recv, sibling).start()
     wait_bytes(right_all.at[:, pl.ds(0, 8)], sibling_recv)
-    wait_bytes(edge_all.at[pl.ds(0, 3)], recv_sem.at[2])
-
-    def send_mixed(i, px, py, pxy):
-        remote(
-            mixed_send.at[i, pxy], mixed_all.at[z * 16 + xy], send_sem.at[7], recv_sem.at[7],
-            device_at(px, py, z_peers[i], core),
-        ).start()
+
+    def send_mixed(part):
+        def start(i, px, py, pxy):
+            remote(
+                mixed_send.at[part, i, pxy], mixed_all.at[part, z * 16 + xy],
+                send_sem.at[7], mixed_recv.at[part], device_at(px, py, z_peers[i], core),
+            ).start()
+
+        return start
 
     for group in GROUPS:
         first, count = group[0], len(group)
@@ -303,55 +310,60 @@
         left = jnp.concatenate(
             [rows_of(left_all[step, pl.ds(first, count)]) for step in range(4)], axis=1
         )
-        for part in range(4):
-            right = jnp.concatenate([rows_of(right_all[part * 4 + step]) for step in range(4)], axis=1)
+        for column in range(4):
+            right = jnp.concatenate([rows_of(right_all[column * 4 + step]) for step in range(4)], axis=1)
             total = lax.dot_general(left, right, NT, preferred_element_type=F32)
-            total = total.reshape(count, 4, 8, 128).astype(BF16)
+            total = total.reshape(count, 4, 8, 128)
             for py in range(4):
-                mixed_send[pl.ds(first, count), py * 4 + part] = total[:, py]
-        to_all(send_mixed, group)
-    own(mixed_send.at[7, xy], mixed_all.at[z * 16 + xy], 2).wait()
-    wait_bytes(mixed_all.at[pl.ds(0, 127)], recv_sem.at[7])
-
-    centred(mixed_all, wide)
+                for part in range(2):
+                    mixed_send[part, pl.ds(first, count), py * 4 + column] = total[
+                        :, py, part * 4 : part * 4 + 4
+                    ].astype(BF16)
+        to_all(send_mixed(0), group)
+    to_all(send_mixed(1), range(8))
+    own_mixed = [own(mixed_send.at[part, 7, xy], mixed_all.at[part, z * 16 + xy], 2 + part) for part in range(2)]
+
+    wait_bytes(edge_all.at[pl.ds(0, 3)], recv_sem.at[2])
     edge_sum = edge_all[0] + edge_all[1] + edge_all[2] + edge_all[3]
     out_gain = jnp.transpose(jnp.broadcast_to(edge_sum[0:1], (128, 128)))
     out_shift = jnp.transpose(jnp.broadcast_to(edge_sum[1:2], (128, 128)))
 
-    def finish(step, _):
-        normed = []
-        for member in range(2):
-            r = step * 2 + member
-            value = wide[pl.ds(r, 128, stride=8), :] * out_gain + out_shift
-            normed.append(value.astype(BF16))
-        projected = jnp.dot(
-            w_out_t[...], jnp.concatenate(normed, axis=1), preferred_element_type=F32
-        )
-        for member in range(2):
-            at = pl.ds(pl.multiple_of((step * 2 + member) * 128, 128), 128)
-            left_f[at, :] = gate_f[at, :] * projected[:, member * 128 : member * 128 + 128]
-        return 0
-
-    lax.fori_loop(0, 4, finish, 0, unroll=True)
-
-    for t in (2, 1, 3, 0):
-        ph = hi_peer(t)
-        part = out_send.at[pl.ds(ph * 2, 2)]
-        by_channel(left_f, out_send, ph * 2, 2)
-        if t:
-            remote(part, out.at[:, :, z_hi], send_sem.at[8], recv_sem.at[8], at_hi(ph)).start()
-        else:
-            own(part, out.at[:, :, z_hi], 3).wait()
-    wait_bytes(out.at[:, :, pl.ds(0, 3)], recv_sem.at[8])
+    own_out = []
+    for part in range(2):
+        own_mixed[part].wait()
+        wait_bytes(mixed_all.at[part, pl.ds(0, 127)], mixed_recv.at[part])
+        centred(mixed_all.at[part], wide)
+        for step in range(2):
+            normed = []
+            for member in range(2):
+                value = wide[pl.ds(step * 2 + member, 128, stride=4), :] * out_gain + out_shift
+                normed.append(value.astype(BF16))
+            projected = jnp.dot(
+                w_out_t[...], jnp.concatenate(normed, axis=1), preferred_element_type=F32
+            )
+            for member in range(2):
+                at = pl.ds((part * 4 + step * 2 + member) * 128, 128)
+                left_f[at, :] = gate_f[at, :] * projected[:, member * 128 : member * 128 + 128]
+        for t in (2, 1, 3, 0):
+            ph = hi_peer(t)
+            rows, place = out_send.at[part, pl.ds(ph * 2, 2)], out.at[:, :, z_hi, part]
+            by_channel(left_f, out_send.at[part], ph * 2, 2, part * 512)
+            if t:
+                remote(rows, place, send_sem.at[8], out_sem.at[part], at_hi(ph)).start()
+            else:
+                own_out.append(own(rows, place, 4 + part))
+    for part in range(2):
+        own_out[part].wait()
+        wait_bytes(out.at[:, :, pl.ds(0, 3), part], out_sem.at[part])
 
     wait_bytes(xin.at[pl.ds(0, 96)], send_sem.at[0])
     wait_bytes(w_all.at[pl.ds(3, 2), pl.ds(0, 3), pl.ds(0, 2)], send_sem.at[1])
     wait_bytes(edge_all.at[pl.ds(0, 3)], send_sem.at[2])
     wait_bytes(w_all.at[pl.ds(0, 3), :, pl.ds(0, 3)], send_sem.at[3])
     wait_bytes(w_all.at[pl.ds(3, 2), :, pl.ds(0, 2)], send_sem.at[4])
-    wait_bytes(mixed_all.at[pl.ds(0, 127)], send_sem.at[5])
-    wait_bytes(mixed_all.at[pl.ds(0, 127)], send_sem.at[6])
-    wait_bytes(mixed_all.at[pl.ds(0, 127)], send_sem.at[7])
+    wait_bytes(xin.at[pl.ds(0, 127)], send_sem.at[5])
+    wait_bytes(xin.at[pl.ds(0, 127)], send_sem.at[6])
+    wait_bytes(mixed_all.at[:, pl.ds(0, 127)], send_sem.at[7])
     wait_bytes(out.at[:, :, pl.ds(0, 3)], send_sem.at[8])
     wait_bytes(w_all.at[pl.ds(0, 3), pl.ds(0, 3), 0], send_sem.at[9])
     wait_bytes(right_all.at[:, pl.ds(0, 8)], sibling_send)
@@ -393,7 +405,7 @@
     result = pl.pallas_call(
         kernel,
         name="triangle",
-        out_shape=pltpu.VMEM((2, 16, 4, 8, 128), BF16),
+        out_shape=pltpu.VMEM((2, 16, 4, 2, 4, 128), BF16),
         in_specs=[any_spec] * 13,
         out_specs=pl.BlockSpec(memory_space=pl.ANY),
         scratch_shapes=[
@@ -417,17 +429,19 @@
             pltpu.VMEM((4, 8, 4, 8, 128), BF16),
             pltpu.VMEM((8, 16, 8, 128), BF16),
             pltpu.VMEM((16, 16, 8, 128), BF16),
-            pltpu.VMEM((8, 16, 8, 128), BF16),
-            pltpu.VMEM((128, 8, 128), BF16),
-            pltpu.VMEM((8, 16, 8, 128), BF16),
+            pltpu.VMEM((2, 8, 16, 4, 128), BF16),
+            pltpu.VMEM((2, 128, 4, 128), BF16),
+            pltpu.VMEM((2, 8, 16, 4, 128), BF16),
             pltpu.SemaphoreType.DMA((13,)),
             pltpu.SemaphoreType.DMA((10,)),
             pltpu.SemaphoreType.DMA((10,)),
-            pltpu.SemaphoreType.DMA((4,)),
+            pltpu.SemaphoreType.DMA((6,)),
             pltpu.SemaphoreType.DMA,
             pltpu.SemaphoreType.DMA((8,)),
             pltpu.SemaphoreType.DMA((8,)),
             pltpu.SemaphoreType.DMA,
+            pltpu.SemaphoreType.DMA((2,)),
+            pltpu.SemaphoreType.DMA((2,)),
             pltpu.SemaphoreType.REGULAR,
         ],
         compiler_params=pltpu.CompilerParams(

time: 52 us -> 51.3 us (0.987)
  Pallas kernels: 51.2 us -> 50.4 us
    pallas_call x1, Pallas kernels: 51.2 us -> 50.4 us  [on_device(): pl.pallas_call(kernel, name='triangle', out_shape=pltpu.VMEM((2, 16, 4, 2...]
where the time goes in v5:
time: 51.3 us; the launch traced here: 51.1 us
  Pallas kernels  50.4 us (98%)
  local copies, waits for them, and re-layouts  0.71 us (1%)
    pallas_call x1, Pallas kernels, on_device(): pl.pallas_call(kernel, name='triangle', out_shape=pltpu.VMEM((2, 16, 4, 2...  50.4 us

profile of v5, /device:TPU:1, one launch (start us, length us, event | category | flops | bytes accessed | tf_op | source)
XLA Modules:
  0.0 51.1 jit_solution(3858217925102596825)
XLA Ops:
  0.0 50.4 %triangle.1 = bf16[2,16,4,2,4,128]{5,4,3,2,1,0:T(4,128)(2,1)S(1)} custom-call(bf16[32,4,8,128]{3,2,1,0:T(8,128)(2,1)} %bitcast.19, s32[4,128]{1,0:T(4,128)} %bitcast.25, s32[512]{0:T(512)} %valid_s_in.1, f32[128]{0:T(128)} %gain_in.1, f32[128]{0:T(128)} %bias_in.1, bf16[4,8,128]{2,1,0:T(8,128)(2,1)} %bitcast.20, bf16[4,8,128]{2,1,0:T(8,128)(2,1)} %bitcast.21, ...), custom_call_target="tpu_custom_call" | custom-call | tf_op jit(solution)/shard_map/triangle/pallas_call | solution.py:405
  50.4 0.7 %copy.14 = bf16[32,32,128]{2,1,0:T(8,128)(2,1)} copy(bf16[32,32,128]{2,1,0:T(8,128)(2,1)S(1)} %bitcast.18) | data formatting | bytes 524288

commit v6 on v5

--- a/solution.py
+++ b/solution.py
@@ -119,14 +119,10 @@
     lax.fori_loop(1, 16, greet_xy, 0)
     pl.semaphore_signal(barrier, inc=1, device_id=sibling, device_id_type=MESH)
 
-    half = pl.ds(core * 2, 2)
     own_rows = pltpu.make_async_copy(pair.at[:, z_hi], xin.at[pl.ds(z_hi * 32, 32)], load_sem.at[0])
     weight_loads = [
         pltpu.make_async_copy(w.at[x], w_all.at[t, z_hi, x], load_sem.at[1 + t])
-        for t, w in enumerate((w0, w1, w2))
-    ] + [
-        pltpu.make_async_copy(w.at[half], w_all.at[3 + t, z_hi, half], load_sem.at[4 + t])
-        for t, w in enumerate((w3, w4))
+        for t, w in enumerate((w0, w1, w2, w3, w4))
     ]
     out_loads = [
         pltpu.make_async_copy(w_out_in, w_out_v, load_sem.at[6]),
@@ -158,11 +154,7 @@
 
     pl.semaphore_wait(barrier, 23)
 
-    right_weights = w_all.at[pl.ds(3, 2), z_hi, half]
-    left_weights = w_all.at[pl.ds(0, 3), z_hi, x]
-    for t in (2, 1, 3):
-        ph = hi_peer(t)
-        remote(right_weights, right_weights, send_sem.at[1], recv_sem.at[1], at_hi(ph)).start()
+    left_weights = w_all.at[:, z_hi, x]
     for t in (2, 1, 3):
         ph = hi_peer(t)
         remote(left_weights, left_weights, send_sem.at[9], recv_sem.at[9], at_hi(ph)).start()
@@ -180,11 +172,8 @@
         remote(edge, edge_all.at[z_hi], send_sem.at[2], recv_sem.at[2], at_hi(ph)).start()
     for copy in in_loads:
         copy.wait()
-    wait_bytes(w_all.at[pl.ds(3, 2), pl.ds(0, 3), pl.ds(0, 2)], recv_sem.at[1])
-    right_weights = w_all.at[pl.ds(3, 2), :, half]
-    remote(right_weights, right_weights, send_sem.at[4], recv_sem.at[4], sibling).start()
-    wait_bytes(w_all.at[pl.ds(0, 3), pl.ds(0, 3), 0], recv_sem.at[9])
-    left_weights = w_all.at[pl.ds(0, 3), :, x]
+    wait_bytes(w_all.at[:, pl.ds(0, 3), 0], recv_sem.at[9])
+    left_weights = w_all.at[:, :, x]
     for t in (2, 1, 3):
         remote(
             left_weights, left_weights, send_sem.at[3], recv_sem.at[3],
@@ -195,7 +184,7 @@
     wait_bytes(xin.at[pl.ds(0, 96)], recv_sem.at[0])
     centred(xin, wide, gain_s, bias_s)
 
-    wait_bytes(w_all.at[pl.ds(3, 2), :, pl.ds(0, 2)], recv_sem.at[4])
+    wait_bytes(w_all.at[:, :, pl.ds(0, 3)], recv_sem.at[3])
     col_valid = valid_v[pl.ds(x, 1), :].astype(F32)
     first_row = row * 32 + z_hi * 8
 
@@ -267,7 +256,6 @@
     to_all(send_right, range(8), lambda pz: by_channel(right_f, right_send, pz, 1))
     own_right = own(right_send.at[z, xy], right_all.at[xy, mine], 0)
 
-    wait_bytes(w_all.at[pl.ds(0, 3), :, pl.ds(0, 3)], recv_sem.at[3])
     edges(0, left_f)
 
     def send_left(i, px, py, pxy):
@@ -357,15 +345,13 @@
         wait_bytes(out.at[:, :, pl.ds(0, 3), part], out_sem.at[part])
 
     wait_bytes(xin.at[pl.ds(0, 96)], send_sem.at[0])
-    wait_bytes(w_all.at[pl.ds(3, 2), pl.ds(0, 3), pl.ds(0, 2)], send_sem.at[1])
     wait_bytes(edge_all.at[pl.ds(0, 3)], send_sem.at[2])
-    wait_bytes(w_all.at[pl.ds(0, 3), :, pl.ds(0, 3)], send_sem.at[3])
-    wait_bytes(w_all.at[pl.ds(3, 2), :, pl.ds(0, 2)], send_sem.at[4])
+    wait_bytes(w_all.at[:, :, pl.ds(0, 3)], send_sem.at[3])
     wait_bytes(xin.at[pl.ds(0, 127)], send_sem.at[5])
     wait_bytes(xin.at[pl.ds(0, 127)], send_sem.at[6])
     wait_bytes(mixed_all.at[:, pl.ds(0, 127)], send_sem.at[7])
     wait_bytes(out.at[:, :, pl.ds(0, 3)], send_sem.at[8])
-    wait_bytes(w_all.at[pl.ds(0, 3), pl.ds(0, 3), 0], send_sem.at[9])
+    wait_bytes(w_all.at[:, pl.ds(0, 3), 0], send_sem.at[9])
     wait_bytes(right_all.at[:, pl.ds(0, 8)], sibling_send)
 
 

time: 51.3 us -> 50.8 us (level)
  the two profiles are of different devices: /device:TPU:1 before, /device:TPU:32 now
where the time goes in v6:
time: 50.8 us; the launch traced here: 50.7 us
  Pallas kernels  49.9 us (98%)
  local copies, waits for them, and re-layouts  0.71 us (1%)
    pallas_call x1, Pallas kernels, on_device(): pl.pallas_call(kernel, name='triangle', out_shape=pltpu.VMEM((2, 16, 4, 2...  49.9 us

profile of v6, /device:TPU:32, one launch (start us, length us, event | category | flops | bytes accessed | tf_op | source)
XLA Modules:
  0.0 50.7 jit_solution(667496354581894664)
XLA Ops:
  0.0 49.9 %triangle.1 = bf16[2,16,4,2,4,128]{5,4,3,2,1,0:T(4,128)(2,1)S(1)} custom-call(bf16[32,4,8,128]{3,2,1,0:T(8,128)(2,1)} %bitcast.19, s32[4,128]{1,0:T(4,128)} %bitcast.25, s32[512]{0:T(512)} %valid_s_in.1, f32[128]{0:T(128)} %gain_in.1, f32[128]{0:T(128)} %bias_in.1, bf16[4,8,128]{2,1,0:T(8,128)(2,1)} %bitcast.20, bf16[4,8,128]{2,1,0:T(8,128)(2,1)} %bitcast.21, ...), custom_call_target="tpu_custom_call" | custom-call | tf_op jit(solution)/shard_map/triangle/pallas_call | solution.py:391
  49.9 0.7 %copy.14 = bf16[32,32,128]{2,1,0:T(8,128)(2,1)} copy(bf16[32,32,128]{2,1,0:T(8,128)(2,1)S(1)} %bitcast.18) | data formatting | bytes 524288

commit v7 on v6

--- a/solution.py
+++ b/solution.py
@@ -39,28 +39,27 @@
     return (second == first + offset).astype(F32).astype(BF16)
 
 
-def centred(blocks, scratch, gain=None, shift=None):
+def sums(blocks, shift, first, count):
+    def add(step, totals):
+        part = blocks[pl.ds(first + step * 16, 16)].astype(F32) - shift
+        return totals[0] + jnp.sum(part, axis=0), totals[1] + jnp.sum(part * part, axis=0)
+
+    zero = jnp.zeros(blocks.shape[1:], F32)
+    return lax.fori_loop(0, count // 16, add, (zero, zero))
+
+
+def centred(blocks, scratch, total, square, shift, gain=None, offset=None):
     n = blocks.shape[1]
-
-    def add(step, total):
-        part = blocks[pl.ds(step * 16, 16)].astype(F32)
-        return total + jnp.sum(part, axis=0)
-
-    centre = lax.fori_loop(0, 8, add, jnp.zeros((n, 128), F32)) * (1.0 / 128)
-
-    def add_square(step, total):
-        part = blocks[pl.ds(step * 16, 16)].astype(F32) - centre
-        return total + jnp.sum(part * part, axis=0)
-
-    spread = lax.fori_loop(0, 8, add_square, jnp.zeros((n, 128), F32)) * (1.0 / 128)
-    scale = lax.rsqrt(spread + EPSILON)
+    above = total * (1.0 / 128)
+    spread = square * (1.0 / 128) - above * above
+    centre, scale = shift + above, lax.rsqrt(spread + EPSILON)
 
     def put(step, _):
         for member in range(16):
             c = step * 16 + member
             value = (blocks[c].astype(F32) - centre) * scale
             if gain is not None:
-                value = value * gain[c] + shift[c]
+                value = value * gain[c] + offset[c]
             scratch[pl.ds(pl.multiple_of(c * n, n), n), :] = value
         return 0
 
@@ -85,7 +84,7 @@
     edge, edge_all,
     wide, left_f, right_f, gate_f,
     left_send, left_all, right_send, right_all, mixed_send, mixed_all, out_send,
-    load_sem, send_sem, recv_sem, own_sem, sibling_send, left_recv, right_recv, sibling_recv, mixed_recv, out_sem, plane_sem,
+    load_sem, send_sem, recv_sem, own_sem, sibling_send, left_recv, right_recv, sibling_recv, xin_sem, mixed_recv, out_sem, plane_sem,
 ):
     row, x, z_hi = lax.axis_index("row"), lax.axis_index("col"), lax.axis_index("chan")
     core, z_lo, y = row % 2, (row // 2) % 2, row // 4
@@ -161,15 +160,12 @@
     for t in (2, 1, 3):
         ph = hi_peer(t)
         remote(
-            pair.at[:, ph], xin.at[pl.ds(z_hi * 32, 32)], send_sem.at[0], recv_sem.at[0], at_hi(ph)
+            pair.at[:, ph], xin.at[pl.ds(z_hi * 32, 32)], send_sem.at[0], xin_sem.at[t], at_hi(ph)
         ).start()
     for pz in z_peers[:7]:
         pl.semaphore_signal(
             plane_sem, inc=1, device_id=device_at(x, y, pz, core), device_id_type=MESH
         )
-    for t in (2, 1, 3):
-        ph = hi_peer(t)
-        remote(edge, edge_all.at[z_hi], send_sem.at[2], recv_sem.at[2], at_hi(ph)).start()
     for copy in in_loads:
         copy.wait()
     wait_bytes(w_all.at[:, pl.ds(0, 3), 0], recv_sem.at[9])
@@ -181,8 +177,14 @@
         ).start()
 
     own_rows.wait()
-    wait_bytes(xin.at[pl.ds(0, 96)], recv_sem.at[0])
-    centred(xin, wide, gain_s, bias_s)
+    own_total, _ = sums(xin, 0.0, z_hi * 32, 32)
+    shift = own_total * (1.0 / 32)
+    total, square = sums(xin, shift, z_hi * 32, 32)
+    for t in (1, 3, 2):
+        wait_bytes(xin.at[pl.ds(0, 32)], xin_sem.at[t])
+        more = sums(xin, shift, hi_peer(4 - t) * 32, 32)
+        total, square = total + more[0], square + more[1]
+    centred(xin, wide, total, square, shift, gain_s, bias_s)
 
     wait_bytes(w_all.at[:, :, pl.ds(0, 3)], recv_sem.at[3])
     col_valid = valid_v[pl.ds(x, 1), :].astype(F32)
@@ -192,8 +194,8 @@
         normed = [wide[pl.ds(step * 2 + member, 128, stride=8), :].astype(BF16) for member in range(2)]
         return jnp.concatenate(normed, axis=1)
 
-    def linear(t, normed):
-        return jnp.dot(rows_of(w_all[t]), normed, preferred_element_type=F32)
+    def linear(weight, normed):
+        return jnp.dot(weight, normed, preferred_element_type=F32)
 
     def put_rows(ref, step, value):
         for member in range(2):
@@ -201,19 +203,21 @@
             ref[at, :] = value[:, member * 128 : member * 128 + 128]
 
     def edges(first, ref):
+        gate_rows, value_rows = rows_of(w_all[first]), rows_of(w_all[first + 1])
+
         def project(step, _):
             normed = rows_at(step)
             masks = [
                 col_valid * valid_s[first_row + step * 2 + member].astype(F32) for member in range(2)
             ]
-            value = jax.nn.sigmoid(linear(first, normed)) * linear(first + 1, normed)
+            value = jax.nn.sigmoid(linear(gate_rows, normed)) * linear(value_rows, normed)
             put_rows(ref, step, value * jnp.concatenate(masks, axis=1))
             return 0
 
         lax.fori_loop(0, 4, project, 0, unroll=True)
 
     def gates(step, _):
-        value = jax.nn.sigmoid(linear(2, rows_at(step)))
+        value = jax.nn.sigmoid(linear(rows_of(w_all[2]), rows_at(step)))
         put_rows(gate_f, step, value.astype(BF16).astype(F32))
         return 0
 
@@ -266,6 +270,9 @@
 
     to_all(send_left, range(8), lambda pz: by_channel(left_f, left_send, pz, 1))
     own_left = own(left_send.at[z, xy], left_all.at[x, 7, y], 1)
+    for t in (2, 1, 3):
+        ph = hi_peer(t)
+        remote(edge, edge_all.at[z_hi], send_sem.at[2], recv_sem.at[2], at_hi(ph)).start()
     lax.fori_loop(0, 4, gates, 0, unroll=True)
 
     for i in range(8):
@@ -320,7 +327,7 @@
     for part in range(2):
         own_mixed[part].wait()
         wait_bytes(mixed_all.at[part, pl.ds(0, 127)], mixed_recv.at[part])
-        centred(mixed_all.at[part], wide)
+        centred(mixed_all.at[part], wide, *sums(mixed_all.at[part], 0.0, 0, 128), 0.0)
         for step in range(2):
             normed = []
             for member in range(2):
@@ -426,6 +433,7 @@
             pltpu.SemaphoreType.DMA((8,)),
             pltpu.SemaphoreType.DMA((8,)),
             pltpu.SemaphoreType.DMA,
+            pltpu.SemaphoreType.DMA((4,)),
             pltpu.SemaphoreType.DMA((2,)),
             pltpu.SemaphoreType.DMA((2,)),
             pltpu.SemaphoreType.REGULAR,

time: 50.8 us -> 51.8 us (1.020)
  the two profiles are of different devices: /device:TPU:32 before, /device:TPU:1 now
where the time goes in v7:
time: 51.8 us; the launch traced here: 51.7 us
  Pallas kernels  50.9 us (98%)
  local copies, waits for them, and re-layouts  0.71 us (1%)
    pallas_call x1, Pallas kernels, on_device(): pl.pallas_call(kernel, name='triangle', out_shape=pltpu.VMEM((2, 16, 4, 2...  50.9 us

profile of v7, /device:TPU:1, one launch (start us, length us, event | category | flops | bytes accessed | tf_op | source)
XLA Modules:
  0.0 51.7 jit_solution(15056382372218243216)
XLA Ops:
  0.0 50.9 %triangle.1 = bf16[2,16,4,2,4,128]{5,4,3,2,1,0:T(4,128)(2,1)S(1)} custom-call(bf16[32,4,8,128]{3,2,1,0:T(8,128)(2,1)} %bitcast.19, s32[4,128]{1,0:T(4,128)} %bitcast.25, s32[512]{0:T(512)} %valid_s_in.1, f32[128]{0:T(128)} %gain_in.1, f32[128]{0:T(128)} %bias_in.1, bf16[4,8,128]{2,1,0:T(8,128)(2,1)} %bitcast.20, bf16[4,8,128]{2,1,0:T(8,128)(2,1)} %bitcast.21, ...), custom_call_target="tpu_custom_call" | custom-call | tf_op jit(solution)/shard_map/triangle/pallas_call | solution.py:398
  51.0 0.7 %copy.14 = bf16[32,32,128]{2,1,0:T(8,128)(2,1)} copy(bf16[32,32,128]{2,1,0:T(8,128)(2,1)S(1)} %bitcast.18) | data formatting | bytes 524288
